TPU v7x, 32 devices: a whole 2x2x4 slice. The times are simulated.
32 devices in a mesh: member: 2 (over y), comp: 4 (over z), lev: 4 (over x, core).
Axes of the slice: x: 2, y: 2, z: 4, core: 2. Of those that a mesh axis runs over, the one named last changes fastest.
Arguments:
- atm_state: float32 [144, 64, 512], P('member', 'comp', 'lev'), parts along dimension 0, may hold values from -6 to 6
- ocean_state: float32 [120, 64, 1024], P('member', 'comp', 'lev'), parts along dimension 0, may hold values from -6 to 6
- flux_prev: bfloat16 [16, 64, 512], P('member', 'comp', 'lev'), parts along dimension 0, may hold values from -6 to 6
- pair_offset: int32 [2048], P(('comp', 'lev')), may hold values from 0 to 8, as said below
- pair_tile: int32 [2048], P(('comp', 'lev')), may hold values from 0 to 15
- pair_weight: bfloat16 [2048, 128, 256], P(('comp', 'lev')), may hold values from 0.0019989014 to 0.019897461
- atm_mix: float32 [72, 72], replicated, may hold values from 0 to 1
- ocean_mix: float32 [60, 60], replicated, may hold values from 0 to 1
- exchange_response_matrix: float32 [8, 72], replicated, may hold values from -0.75 to 0.75
- exchange_factor_array: float32 [8], replicated, may hold values from 0.5 to 2
- depth_profile: float32 [60, 8], replicated, may hold values from -2 to 2
- sea_mask: int32 [64, 1024], P('comp', 'lev'), may hold values 0 or 1
Outputs:
- atm_next: float32 [144, 64, 512], P('member', 'comp', 'lev'), parts along dimension 0
- ocean_next: float32 [120, 64, 1024], P('member', 'comp', 'lev'), parts along dimension 0
- flux_next: bfloat16 [16, 64, 512], P('member', 'comp', 'lev'), parts along dimension 0
There are 2 independent parts, one for each index of `member`. A program takes and returns all parts, laid end to end along the dimension named above; an argument that names none is the same for every part. Nothing has to cross between parts.
Inputs may be any that keep to these rules, and one draw needn't show every extreme that they name: `pair_offset`: among the 128 pairs of one block, offset 4 (the block itself) appears 128 / 4 times, each of 1, 3, 5, 7 * 128 / 8 times and each of 0, 2, 6, 8 * 128 / 16 times; offset d stands for the block d // 3 - 1 rows and d % 3 - 1 columns of blocks away.
All inputs are finite; a program needn't handle non-finite values. No bound on the sum of `sea_mask` on one device may be relied on, other than what follows from the above.
Results may differ from a plain program's by a relative error of at most 0.0049.
Values may be sent and summed in bfloat16 or wider, within the bound.
A program may use at most 64 MiB of HBM per device.

v0:
```python
import jax
import jax.numpy as jnp
from jax import lax
from jax.sharding import PartitionSpec as P

ASTEPS = 4
OSTEPS = 4


atmos_diffusion = 0.24
ocean_diffusion = 0.24
interface_linkage = 0.5


def extended(block, sides, width):
    for axis, dim in sides:
        count = lax.axis_size(axis)
        forward = [(i, i + 1) for i in range(count - 1)]
        backward = [(target, source) for source, target in forward]
        low = lax.ppermute(
            lax.slice_in_dim(block, block.shape[dim] - width, None, axis=dim), axis, forward
        )
        high = lax.ppermute(lax.slice_in_dim(block, 0, width, axis=dim), axis, backward)
        block = jnp.concatenate([low, block, high], axis=dim)
    return block


def spread(padded):
    center = padded[:, 1:-1, 1:-1]
    return (
        padded[:, 2:, 1:-1]
        + padded[:, :-2, 1:-1]
        + padded[:, 1:-1, 2:]
        + padded[:, 1:-1, :-2]
        - 4.0 * center
    )


def column_mix(matrix, field):
    return jnp.einsum("kj,jyx->kyx", matrix, field, precision=lax.Precision.HIGHEST)


def reflect(index, count):
    return jnp.where(
        index < 0, -index, jnp.where(index > count - 1, 2 * (count - 1) - index, index)
    )


def body(
    atm_state,
    ocean_state,
    flux_prev,
    pair_offset,
    pair_tile,
    pair_weight,
    atm_mix,
    ocean_mix,
    exchange_response_matrix,
    exchange_factor_array,
    depth_profile,
    sea_mask,
):
    comp_count = lax.axis_size("comp")
    lev_count = lax.axis_size("lev")
    row_block = lax.axis_index("comp")
    col_block = lax.axis_index("lev")
    pairs = pair_weight.shape[0]
    vertical_air_profile = atm_state.shape[0]
    tiles_atm = atm_state.shape[1]
    cells_atm = atm_state.shape[2]
    tiles_ocean = ocean_state.shape[1]
    cells_ocean = ocean_state.shape[2]
    per_tile = pairs // tiles_atm
    channels = flux_prev.shape[0]
    width = channels * cells_ocean
    dest_row = reflect(row_block + pair_offset // 3 - 1, comp_count)
    dest_col = reflect(col_block + pair_offset % 3 - 1, lev_count)
    near_index = (dest_row - row_block + 1) * 3 + (dest_col - col_block + 1)
    slot = near_index * tiles_ocean + pair_tile
    weights_grid = pair_weight.reshape(tiles_atm, per_tile, cells_atm, cells_ocean)
    products = jnp.einsum(
        "cya,ypao->ypco", flux_prev, weights_grid, preferred_element_type=jnp.float32
    )
    products = products.reshape(pairs, width)
    select = (jnp.arange(9 * tiles_ocean, dtype=jnp.int32)[:, None] == slot[None, :]).astype(
        jnp.float32
    )
    partial_value = jnp.dot(select, products, precision=lax.Precision.HIGHEST).astype(jnp.bfloat16)
    partial_value = partial_value.reshape(3, 3, tiles_ocean, width)
    padded_tiles = extended(partial_value, (("comp", 0), ("lev", 1)), 1)
    incoming = padded_tiles[0::2, 0::2]
    received = jnp.sum(incoming.astype(jnp.float32), axis=(0, 1))
    received = received.reshape(tiles_ocean, channels, cells_ocean).transpose(1, 0, 2)
    surface = ocean_state[0].astype(jnp.bfloat16)
    every_row = lax.all_gather(surface, ("comp", "lev"), axis=0, tiled=True)
    rows = jnp.take(every_row, (dest_row * lev_count + dest_col) * tiles_ocean + pair_tile, axis=0)
    rows = rows.reshape(tiles_atm, per_tile, cells_ocean)
    stacked_rows = jnp.stack([rows, jnp.ones_like(rows)], axis=2)
    panel_totals = jnp.einsum(
        "ypjo,ypao->jya", stacked_rows, weights_grid, preferred_element_type=jnp.float32
    )
    ocean_skin_heat_for_air = panel_totals[0] / panel_totals[1]
    wet = sea_mask.astype(jnp.float32)
    exchange_total = jnp.zeros((channels, tiles_atm, cells_atm), jnp.float32)
    forcing = jnp.einsum("kc,cyx->kyx", depth_profile, received, precision=lax.Precision.HIGHEST)
    ocean = ocean_state
    for step in range(OSTEPS):
        padded = extended(ocean, (("comp", 1), ("lev", 2)), 1)
        ocean = wet * (column_mix(ocean_mix, ocean + ocean_diffusion * spread(padded)) + forcing)
    atmos = atm_state
    for step in range(ASTEPS):
        padded = extended(atmos, (("comp", 1), ("lev", 2)), 1)
        blended_air_profiles = column_mix(atm_mix, atmos + atmos_diffusion * spread(padded))
        thermal_difference = (
            ocean_skin_heat_for_air - blended_air_profiles[vertical_air_profile - 1]
        )
        blended_air_profiles = blended_air_profiles.at[vertical_air_profile - 1].add(
            interface_linkage * thermal_difference
        )
        exchange_total = (
            exchange_total
            + jnp.einsum(
                "jr,rip->jip",
                exchange_response_matrix,
                blended_air_profiles,
                precision=lax.Precision.HIGHEST,
            )
            + exchange_factor_array[:, None, None] * thermal_difference[None]
        )
        atmos = blended_air_profiles
    return (atmos, ocean, (exchange_total / ASTEPS).astype(jnp.bfloat16))


def solution(mesh):
    in_specs = (
        P("member", "comp", "lev"),
        P("member", "comp", "lev"),
        P("member", "comp", "lev"),
        P(("comp", "lev")),
        P(("comp", "lev")),
        P(("comp", "lev"), None, None),
        P(),
        P(),
        P(),
        P(),
        P(),
        P("comp", "lev"),
    )
    out_specs = (P("member", "comp", "lev"), P("member", "comp", "lev"), P("member", "comp", "lev"))
    return jax.shard_map(body, mesh=mesh, in_specs=in_specs, out_specs=out_specs, check_vma=False)
```

profile of v0, /device:TPU:1, one launch (start us, length us, event | category | flops | bytes accessed | tf_op | source)
XLA Modules:
  0.0 242.6 jit_solution(241626225405640545)
XLA Ops:
  1.8 4.0 %collective-permute-start.1 = (f32[72,1,128]{2,1,0:T(1,128)S(1)}, f32[72,1,128]{2,1,0:T(1,128)S(1)}, u32[]{:S(2)}, u32[]{:S(2)}) collective-permute-start(f32[72,1,128]{2,1,0:T(1,128)S(1)} %get-tuple-element.113), channel_id=1, source_target_pairs={{0,4},{4,8},{8,12},{1,5},{5,9},{9,13},{2,6},{6,10},{10,14},{3,7},{... | collective-permute-start | bytes 110600 | tf_op jit(solution)/shard_map/ppermute | solution.py:20
  11.8 5.2 %collective-permute-start.17 = (f32[60,1,256]{2,0,1:T(8,128)}, f32[60,1,256]{2,0,1:T(8,128)}, u32[]{:S(2)}, u32[]{:S(2)}) collective-permute-start(f32[60,1,256]{2,0,1:T(8,128)} %get-tuple-element.82), channel_id=1, source_target_pairs={{0,4},{4,8},{8,12},{1,5},{5,9},{9,13},{2,6},{6,10},{10,14},{3,7},{... | collective-permute-start | bytes 184328 | tf_op jit(solution)/shard_map/ppermute | solution.py:20
  17.9 21.0 %all-gather = bf16[1,256,256]{2,1,0:T(8,128)(2,1)S(1)} all-gather(bf16[1,16,256]{2,1,0:T(8,128)(2,1)S(1)} %slice.521), channel_id=2, replica_groups=mesh['member'=2,'comp'=4,'lev'=4] {'comp','lev'}, dimensions={1}, use_global_device_ids=true | all-gather | bytes 139264 | tf_op jit(solution)/shard_map/all_gather | solution.py:95
  40.1 4.7 %convolution_bitcast_fusion = f32[16,8,8,256]{3,2,1,0:T(8,128)S(1)} fusion(bf16[16,8,128,256]{3,2,1,0:T(8,128)(2,1)} %bitcast.126, bf16[8,16,128,1]{2,1,0,3:T(8,128)(2,1)S(1)} %bitcast.141), kind=kOutput, calls=%fused_computation.12 | convolution fusion | flops 67108864 | bytes 9469952 | tf_op jit(solution)/shard_map/cya,ypao->ypco/dot_general | solution.py:81
  45.8 2.9 %convolution_bitcast_fusion.5 = f32[16,2,128]{2,1,0:T(2,128)} fusion(bf16[16,8,128,256]{3,2,1,0:T(8,128)(2,1)S(1)} %bitcast.127, bf16[16,8,1,256]{3,2,1,0:T(2,128)(2,1)S(1)} %broadcast_select_fusion), kind=kOutput, calls=%fused_computation.33 | convolution fusion | flops 16777216 | bytes 8470528 | tf_op jit(solution)/shard_map/ypjo,ypao->jya/dot_general | solution.py:99
  53.3 2.4 collective-permute-start.2
  72.2 3.1 %collective-permute-start.7 = (f32[72,18,1]{0,2,1:T(1,128)S(1)}, f32[72,18,1]{0,2,1:T(1,128)S(1)}, u32[]{:S(2)}, u32[]{:S(2)}) collective-permute-start(f32[72,18,1]{0,2,1:T(1,128)S(1)} %copy.78), channel_id=1, source_target_pairs={{0,1},{1,2},{2,3},{4,5},{5,6},{6,7},{8,9},{9,10},{10,11},{12,13},{... | collective-permute-start | bytes 15560 | tf_op jit(solution)/shard_map/ppermute | solution.py:20
  79.8 3.6 %collective-permute-start.19 = (f32[60,18,1]{0,2,1:T(1,128)S(1)}, f32[60,18,1]{0,2,1:T(1,128)}, u32[]{:S(2)}, u32[]{:S(2)}) collective-permute-start(f32[60,18,1]{0,2,1:T(1,128)S(1)} %copy.104), channel_id=1, source_target_pairs={{0,1},{1,2},{2,3},{4,5},{5,6},{6,7},{8,9},{9,10},{10,11},{12,13},{... | collective-permute-start | bytes 12968 | tf_op jit(solution)/shard_map/ppermute | solution.py:20
  88.2 2.2 fusion.88
  98.7 4.9 %collective-permute-start.20 = (bf16[1,3,16,2048]{3,2,1,0:T(8,128)(2,1)}, bf16[1,3,16,2048]{3,2,1,0:T(8,128)(2,1)S(1)}, u32[]{:S(2)}, u32[]{:S(2)}) collective-permute-start(bf16[1,3,16,2048]{3,2,1,0:T(8,128)(2,1)} %bitcast.18), channel_id=1, source_target_pairs={{0,4},{4,8},{8,12},{1,5},{5,9},{9,13},{2,6},{6,10},{10,14},{3,7},{... | collective-permute-start | bytes 589832 | tf_op jit(solution)/shard_map/ppermute | solution.py:20
  112.9 4.2 %collective-permute-start.11 = (f32[72,18,1]{0,2,1:T(1,128)}, f32[72,18,1]{0,2,1:T(1,128)}, u32[]{:S(2)}, u32[]{:S(2)}) collective-permute-start(f32[72,18,1]{0,2,1:T(1,128)} %copy.85), channel_id=1, source_target_pairs={{0,1},{1,2},{2,3},{4,5},{5,6},{6,7},{8,9},{9,10},{10,11},{12,13},{... | collective-permute-start | bytes 15560 | tf_op jit(solution)/shard_map/ppermute | solution.py:20
  120.3 2.1 collective-permute-done.10
  126.4 2.2 fusion.82
  130.2 3.6 %collective-permute-start.13 = (f32[72,1,128]{2,1,0:T(1,128)S(1)}, f32[72,1,128]{2,1,0:T(1,128)S(1)}, u32[]{:S(2)}, u32[]{:S(2)}) collective-permute-start(f32[72,1,128]{2,1,0:T(1,128)S(1)} %get-tuple-element.103), channel_id=1, source_target_pairs={{0,4},{4,8},{8,12},{1,5},{5,9},{9,13},{2,6},{6,10},{10,14},{3,7},{... | collective-permute-start | bytes 110600 | tf_op jit(solution)/shard_map/ppermute | solution.py:20
  138.2 2.9 %collective-permute-start.23 = (bf16[5,1,16,2048]{3,2,1,0:T(8,128)(2,1)}, bf16[5,1,16,2048]{3,2,1,0:T(8,128)(2,1)}, u32[]{:S(2)}, u32[]{:S(2)}) collective-permute-start(bf16[5,1,16,2048]{3,2,1,0:T(8,128)(2,1)} %get-tuple-element.84), channel_id=1, source_target_pairs={{1,0},{2,1},{3,2},{5,4},{6,5},{7,6},{9,8},{10,9},{11,10},{13,12},{... | collective-permute-start | bytes 983048 | tf_op jit(solution)/shard_map/ppermute | solution.py:23
  147.5 2.8 %collective-permute-start.15 = (f32[72,18,1]{0,2,1:T(1,128)}, f32[72,18,1]{0,2,1:T(1,128)}, u32[]{:S(2)}, u32[]{:S(2)}) collective-permute-start(f32[72,18,1]{0,2,1:T(1,128)} %copy.92), channel_id=1, source_target_pairs={{0,1},{1,2},{2,3},{4,5},{5,6},{6,7},{8,9},{9,10},{10,11},{12,13},{... | collective-permute-start | bytes 15560 | tf_op jit(solution)/shard_map/ppermute | solution.py:20
  150.2 2.3 collective-permute-start.14
  155.3 2.7 %fusion.7 = f32[60,16,256]{2,0,1:T(8,128)S(1)} fusion(f32[16,256,60]{1,2,0:T(8,128)S(1)} %fusion.117, f32[60,16,256]{2,0,1:T(8,128)S(1)} %copy-done.3, f32[60,18,256]{2,0,1:T(8,128)S(1)} %constant_dynamic-update-slice_fusion, f32[60,18,1]{2,0,1:T(8,128)S(1)} %copy-done.12, f32[60,18,1]{2,0,1:T(8,128)S(1)} %copy-done.11, ...), kind=kOutput, calls=%fused_computation.15 | convolution fusion | flops 180142080 | bytes 4217344 | tf_op jit(solution)/shard_map/kj,jyx->kyx/dot_general | solution.py:40
  159.7 4.3 %collective-permute-start.25 = (f32[60,1,256]{2,0,1:T(8,128)}, f32[60,1,256]{2,0,1:T(8,128)S(1)}, u32[]{:S(2)}, u32[]{:S(2)}) collective-permute-start(f32[60,1,256]{2,0,1:T(8,128)} %get-tuple-element.79), channel_id=1, source_target_pairs={{0,4},{4,8},{8,12},{1,5},{5,9},{9,13},{2,6},{6,10},{10,14},{3,7},{... | collective-permute-start | bytes 184328 | tf_op jit(solution)/shard_map/ppermute | solution.py:20
  175.1 3.9 %collective-permute-start.27 = (f32[60,18,1]{0,2,1:T(1,128)S(1)}, f32[60,18,1]{0,2,1:T(1,128)}, u32[]{:S(2)}, u32[]{:S(2)}) collective-permute-start(f32[60,18,1]{0,2,1:T(1,128)S(1)} %copy.111), channel_id=1, source_target_pairs={{0,1},{1,2},{2,3},{4,5},{5,6},{6,7},{8,9},{9,10},{10,11},{12,13},{... | collective-permute-start | bytes 12968 | tf_op jit(solution)/shard_map/ppermute | solution.py:20
  180.9 2.7 %fusion.76 = f32[72,16,128]{2,1,0:T(8,128)} fusion(f32[72,16,128]{2,1,0:T(8,128)S(1)} %get-tuple-element.96, f32[72,18,1]{2,1,0:T(8,128)} %copy.93, f32[72,1,128]{2,1,0:T(1,128)S(1)} %copy-done.18, f32[72,1,128]{2,1,0:T(1,128)S(1)} %collective-permute-done.13, f32[72,18,1]{2,1,0:T(8,128)S(1)} %copy.91), kind=kLoop, calls=%fused_computation.114 | loop fusion | flops 2211840 | bytes 1263744 | tf_op jit(solution)/shard_map/add | solution.py:113
  187.9 3.2 %fusion.5 = f32[60,16,256]{2,0,1:T(8,128)S(1)} fusion(f32[16,256,60]{1,2,0:T(8,128)S(1)} %copy-done.7, f32[60,16,256]{2,0,1:T(8,128)S(1)} %copy-done.5, f32[60,18,1]{2,0,1:T(8,128)} %copy.112, f32[60,1,256]{2,0,1:T(8,128)} %copy-done.28, f32[60,1,256]{2,0,1:T(8,128)} %copy-done.27, f32[60,18,1]{2,0,1:T(8,128)} %copy.110, f32[16,256]{1,0:T(8,128)S(1)} %copy-done.25, ...), kind=kOutput, calls=%fused_computation.11 | convolution fusion | flops 181125120 | bytes 3111424 | tf_op jit(solution)/shard_map/kj,jyx->kyx/dot_general | solution.py:40
  191.1 3.7 %collective-permute-start.29 = (f32[60,1,256]{2,0,1:T(8,128)S(1)}, f32[60,1,256]{2,0,1:T(8,128)S(1)}, u32[]{:S(2)}, u32[]{:S(2)}) collective-permute-start(f32[60,1,256]{2,0,1:T(8,128)S(1)} %get-tuple-element.77), channel_id=1, source_target_pairs={{0,4},{4,8},{8,12},{1,5},{5,9},{9,13},{2,6},{6,10},{10,14},{3,7},{... | collective-permute-start | bytes 184328 | tf_op jit(solution)/shard_map/ppermute | solution.py:20
  197.1 2.7 %collective-permute-done.28 = f32[60,1,256]{2,0,1:T(8,128)S(1)} collective-permute-done((f32[60,1,256]{2,0,1:T(8,128)S(1)}, f32[60,1,256]{2,0,1:T(8,128)S(1)}, u32[]{:S(2)}, u32[]{:S(2)}) %collective-permute-start.28) | collective-permute-done | bytes 61472 | tf_op jit(solution)/shard_map/ppermute | solution.py:23
  203.7 4.5 %collective-permute-start.31 = (f32[60,18,1]{0,2,1:T(1,128)S(1)}, f32[60,18,1]{0,2,1:T(1,128)S(1)}, u32[]{:S(2)}, u32[]{:S(2)}) collective-permute-start(f32[60,18,1]{0,2,1:T(1,128)S(1)} %copy.115), channel_id=1, source_target_pairs={{0,1},{1,2},{2,3},{4,5},{5,6},{6,7},{8,9},{9,10},{10,11},{12,13},{... | collective-permute-start | bytes 12968 | tf_op jit(solution)/shard_map/ppermute | solution.py:20
  210.2 3.0 %collective-permute-done.30 = f32[60,18,1]{0,2,1:T(1,128)S(1)} collective-permute-done((f32[60,18,1]{0,2,1:T(1,128)S(1)}, f32[60,18,1]{0,2,1:T(1,128)S(1)}, u32[]{:S(2)}, u32[]{:S(2)}) %collective-permute-start.30) | collective-permute-done | bytes 4352 | tf_op jit(solution)/shard_map/ppermute | solution.py:23
  214.7 4.7 %fusion.3 = f32[60,16,256]{2,0,1:T(8,128)S(1)} fusion(f32[16,256,60]{1,2,0:T(8,128)S(1)} %copy-done.7, f32[60,16,256]{2,0,1:T(8,128)} %copy-done.16, f32[60,18,1]{2,0,1:T(8,128)} %copy.116, f32[60,1,256]{2,0,1:T(8,128)S(1)} %collective-permute-done.28, f32[60,1,256]{2,0,1:T(8,128)S(1)} %collective-permute-done.29, f32[60,18,1]{2,0,1:T(8,128)S(1)} %copy.114, ...), kind=kOutput, calls=%fused_computation.8 | convolution fusion | flops 181125120 | bytes 3111424 | tf_op jit(solution)/shard_map/kj,jyx->kyx/dot_general | solution.py:40
  219.5 3.3 %collective-permute-start.33 = (f32[60,1,256]{2,0,1:T(8,128)S(1)}, f32[60,1,256]{2,0,1:T(8,128)S(1)}, u32[]{:S(2)}, u32[]{:S(2)}) collective-permute-start(f32[60,1,256]{2,0,1:T(8,128)S(1)} %get-tuple-element.75), channel_id=1, source_target_pairs={{0,4},{4,8},{8,12},{1,5},{5,9},{9,13},{2,6},{6,10},{10,14},{3,7},{... | collective-permute-start | bytes 184328 | tf_op jit(solution)/shard_map/ppermute | solution.py:20
  224.6 3.1 %collective-permute-done.32 = f32[60,1,256]{2,0,1:T(8,128)S(1)} collective-permute-done((f32[60,1,256]{2,0,1:T(8,128)S(1)}, f32[60,1,256]{2,0,1:T(8,128)S(1)}, u32[]{:S(2)}, u32[]{:S(2)}) %collective-permute-start.32) | collective-permute-done | bytes 61472 | tf_op jit(solution)/shard_map/ppermute | solution.py:23
  229.2 3.5 %collective-permute-start.35 = (f32[60,18,1]{0,2,1:T(1,128)S(1)}, f32[60,18,1]{0,2,1:T(1,128)S(1)}, u32[]{:S(2)}, u32[]{:S(2)}) collective-permute-start(f32[60,18,1]{0,2,1:T(1,128)S(1)} %copy.119), channel_id=1, source_target_pairs={{0,1},{1,2},{2,3},{4,5},{5,6},{6,7},{8,9},{9,10},{10,11},{12,13},{... | collective-permute-start | bytes 12968 | tf_op jit(solution)/shard_map/ppermute | solution.py:20
  232.7 2.2 collective-permute-start.34
  238.3 2.8 %fusion.1 = f32[60,16,256]{2,0,1:T(8,128)S(1)} fusion(f32[16,256,60]{1,2,0:T(8,128)S(1)} %copy-done.7, f32[60,16,256]{2,0,1:T(8,128)S(1)} %copy-done.15, f32[60,18,1]{2,0,1:T(8,128)S(1)} %copy.120, f32[60,1,256]{2,0,1:T(8,128)} %copy-done.29, f32[60,1,256]{2,0,1:T(8,128)S(1)} %collective-permute-done.33, f32[60,18,1]{2,0,1:T(8,128)S(1)} %copy.118, ...), kind=kOutput, calls=%fused_computation.5 | convolution fusion | flops 181125120 | bytes 3111424 | tf_op jit(solution)/shard_map/kj,jyx->kyx/dot_general | solution.py:40
  (234 shorter events, 116.3 us)
Async XLA Ops:
  1.8 47.3 %collective-permute-start.1 = (f32[72,1,128]{2,1,0:T(1,128)S(1)}, f32[72,1,128]{2,1,0:T(1,128)S(1)}, u32[]{:S(2)}, u32[]{:S(2)}) collective-permute-start(f32[72,1,128]{2,1,0:T(1,128)S(1)} %get-tuple-element.113), channel_id=1, source_target_pairs={{0,4},{4,8},{8,12},{1,5},{5,9},{9,13},{2,6},{6,10},{10,14},{3,7},{... | collective-permute-start | bytes 110600 | tf_op jit(solution)/shard_map/ppermute | solution.py:20
  5.8 43.3 %collective-permute-start = (f32[72,1,128]{2,1,0:T(1,128)S(1)}, f32[72,1,128]{2,1,0:T(1,128)S(1)}, u32[]{:S(2)}, u32[]{:S(2)}) collective-permute-start(f32[72,1,128]{2,1,0:T(1,128)S(1)} %get-tuple-element.114), channel_id=1, source_target_pairs={{4,0},{8,4},{12,8},{5,1},{9,5},{13,9},{6,2},{10,6},{14,10},{7,3},{... | collective-permute-start | bytes 110600 | tf_op jit(solution)/shard_map/ppermute | solution.py:23
  10.5 55.3 %collective-permute-start.16 = (f32[60,1,256]{2,0,1:T(8,128)}, f32[60,1,256]{2,0,1:T(8,128)S(1)}, u32[]{:S(2)}, u32[]{:S(2)}) collective-permute-start(f32[60,1,256]{2,0,1:T(8,128)} %get-tuple-element.81), channel_id=1, source_target_pairs={{4,0},{8,4},{12,8},{5,1},{9,5},{13,9},{6,2},{10,6},{14,10},{7,3},{... | collective-permute-start | bytes 184328 | tf_op jit(solution)/shard_map/ppermute | solution.py:23
  11.8 52.5 %collective-permute-start.17 = (f32[60,1,256]{2,0,1:T(8,128)}, f32[60,1,256]{2,0,1:T(8,128)}, u32[]{:S(2)}, u32[]{:S(2)}) collective-permute-start(f32[60,1,256]{2,0,1:T(8,128)} %get-tuple-element.82), channel_id=1, source_target_pairs={{0,4},{4,8},{8,12},{1,5},{5,9},{9,13},{2,6},{6,10},{10,14},{3,7},{... | collective-permute-start | bytes 184328 | tf_op jit(solution)/shard_map/ppermute | solution.py:20
  51.4 7.5 %collective-permute-start.3 = (f32[72,18,1]{0,2,1:T(1,128)S(1)}, f32[72,18,1]{0,2,1:T(1,128)S(1)}, u32[]{:S(2)}, u32[]{:S(2)}) collective-permute-start(f32[72,18,1]{0,2,1:T(1,128)S(1)} %copy.70), channel_id=1, source_target_pairs={{0,1},{1,2},{2,3},{4,5},{5,6},{6,7},{8,9},{9,10},{10,11},{12,13},{... | collective-permute-start | bytes 15560 | tf_op jit(solution)/shard_map/ppermute | solution.py:20
  53.3 5.2 %collective-permute-start.2 = (f32[72,18,1]{0,2,1:T(1,128)}, f32[72,18,1]{0,2,1:T(1,128)S(1)}, u32[]{:S(2)}, u32[]{:S(2)}) collective-permute-start(f32[72,18,1]{0,2,1:T(1,128)} %copy.68), channel_id=1, source_target_pairs={{1,0},{2,1},{3,2},{5,4},{6,5},{7,6},{9,8},{10,9},{11,10},{13,12},{... | collective-permute-start | bytes 15560 | tf_op jit(solution)/shard_map/ppermute | solution.py:23
  72.2 14.7 %collective-permute-start.7 = (f32[72,18,1]{0,2,1:T(1,128)S(1)}, f32[72,18,1]{0,2,1:T(1,128)S(1)}, u32[]{:S(2)}, u32[]{:S(2)}) collective-permute-start(f32[72,18,1]{0,2,1:T(1,128)S(1)} %copy.78), channel_id=1, source_target_pairs={{0,1},{1,2},{2,3},{4,5},{5,6},{6,7},{8,9},{9,10},{10,11},{12,13},{... | collective-permute-start | bytes 15560 | tf_op jit(solution)/shard_map/ppermute | solution.py:20
  75.3 10.3 %collective-permute-start.6 = (f32[72,18,1]{0,2,1:T(1,128)S(1)}, f32[72,18,1]{0,2,1:T(1,128)S(1)}, u32[]{:S(2)}, u32[]{:S(2)}) collective-permute-start(f32[72,18,1]{0,2,1:T(1,128)S(1)} %copy.76), channel_id=1, source_target_pairs={{1,0},{2,1},{3,2},{5,4},{6,5},{7,6},{9,8},{10,9},{11,10},{13,12},{... | collective-permute-start | bytes 15560 | tf_op jit(solution)/shard_map/ppermute | solution.py:23
  79.8 25.6 %collective-permute-start.19 = (f32[60,18,1]{0,2,1:T(1,128)S(1)}, f32[60,18,1]{0,2,1:T(1,128)}, u32[]{:S(2)}, u32[]{:S(2)}) collective-permute-start(f32[60,18,1]{0,2,1:T(1,128)S(1)} %copy.104), channel_id=1, source_target_pairs={{0,1},{1,2},{2,3},{4,5},{5,6},{6,7},{8,9},{9,10},{10,11},{12,13},{... | collective-permute-start | bytes 12968 | tf_op jit(solution)/shard_map/ppermute | solution.py:20
  83.5 14.6 %collective-permute-start.18 = (f32[60,18,1]{0,2,1:T(1,128)S(1)}, f32[60,18,1]{0,2,1:T(1,128)S(1)}, u32[]{:S(2)}, u32[]{:S(2)}) collective-permute-start(f32[60,18,1]{0,2,1:T(1,128)S(1)} %copy.102), channel_id=1, source_target_pairs={{1,0},{2,1},{3,2},{5,4},{6,5},{7,6},{9,8},{10,9},{11,10},{13,12},{... | collective-permute-start | bytes 12968 | tf_op jit(solution)/shard_map/ppermute | solution.py:23
  92.7 14.6 %collective-permute-start.9 = (f32[72,1,128]{2,1,0:T(1,128)}, f32[72,1,128]{2,1,0:T(1,128)S(1)}, u32[]{:S(2)}, u32[]{:S(2)}) collective-permute-start(f32[72,1,128]{2,1,0:T(1,128)} %get-tuple-element.107), channel_id=1, source_target_pairs={{0,4},{4,8},{8,12},{1,5},{5,9},{9,13},{2,6},{6,10},{10,14},{3,7},{... | collective-permute-start | bytes 110600 | tf_op jit(solution)/shard_map/ppermute | solution.py:20
  94.1 13.1 %collective-permute-start.8 = (f32[72,1,128]{2,1,0:T(1,128)}, f32[72,1,128]{2,1,0:T(1,128)S(1)}, u32[]{:S(2)}, u32[]{:S(2)}) collective-permute-start(f32[72,1,128]{2,1,0:T(1,128)} %get-tuple-element.108), channel_id=1, source_target_pairs={{4,0},{8,4},{12,8},{5,1},{9,5},{13,9},{6,2},{10,6},{14,10},{7,3},{... | collective-permute-start | bytes 110600 | tf_op jit(solution)/shard_map/ppermute | solution.py:23
  96.2 39.0 %collective-permute-start.21 = (bf16[1,3,16,2048]{3,2,1,0:T(8,128)(2,1)}, bf16[1,3,16,2048]{3,2,1,0:T(8,128)(2,1)S(1)}, u32[]{:S(2)}, u32[]{:S(2)}) collective-permute-start(bf16[1,3,16,2048]{3,2,1,0:T(8,128)(2,1)} %bitcast.20), channel_id=1, source_target_pairs={{4,0},{8,4},{12,8},{5,1},{9,5},{13,9},{6,2},{10,6},{14,10},{7,3},{... | collective-permute-start | bytes 589832 | tf_op jit(solution)/shard_map/ppermute | solution.py:23
  98.7 36.5 %collective-permute-start.20 = (bf16[1,3,16,2048]{3,2,1,0:T(8,128)(2,1)}, bf16[1,3,16,2048]{3,2,1,0:T(8,128)(2,1)S(1)}, u32[]{:S(2)}, u32[]{:S(2)}) collective-permute-start(bf16[1,3,16,2048]{3,2,1,0:T(8,128)(2,1)} %bitcast.18), channel_id=1, source_target_pairs={{0,4},{4,8},{8,12},{1,5},{5,9},{9,13},{2,6},{6,10},{10,14},{3,7},{... | collective-permute-start | bytes 589832 | tf_op jit(solution)/shard_map/ppermute | solution.py:20
  112.9 11.5 %collective-permute-start.11 = (f32[72,18,1]{0,2,1:T(1,128)}, f32[72,18,1]{0,2,1:T(1,128)}, u32[]{:S(2)}, u32[]{:S(2)}) collective-permute-start(f32[72,18,1]{0,2,1:T(1,128)} %copy.85), channel_id=1, source_target_pairs={{0,1},{1,2},{2,3},{4,5},{5,6},{6,7},{8,9},{9,10},{10,11},{12,13},{... | collective-permute-start | bytes 15560 | tf_op jit(solution)/shard_map/ppermute | solution.py:20
  117.1 5.3 %collective-permute-start.10 = (f32[72,18,1]{0,2,1:T(1,128)}, f32[72,18,1]{0,2,1:T(1,128)}, u32[]{:S(2)}, u32[]{:S(2)}) collective-permute-start(f32[72,18,1]{0,2,1:T(1,128)} %copy.83), channel_id=1, source_target_pairs={{1,0},{2,1},{3,2},{5,4},{6,5},{7,6},{9,8},{10,9},{11,10},{13,12},{... | collective-permute-start | bytes 15560 | tf_op jit(solution)/shard_map/ppermute | solution.py:23
  130.2 10.9 %collective-permute-start.13 = (f32[72,1,128]{2,1,0:T(1,128)S(1)}, f32[72,1,128]{2,1,0:T(1,128)S(1)}, u32[]{:S(2)}, u32[]{:S(2)}) collective-permute-start(f32[72,1,128]{2,1,0:T(1,128)S(1)} %get-tuple-element.103), channel_id=1, source_target_pairs={{0,4},{4,8},{8,12},{1,5},{5,9},{9,13},{2,6},{6,10},{10,14},{3,7},{... | collective-permute-start | bytes 110600 | tf_op jit(solution)/shard_map/ppermute | solution.py:20
  133.9 7.3 %collective-permute-start.12 = (f32[72,1,128]{2,1,0:T(1,128)S(1)}, f32[72,1,128]{2,1,0:T(1,128)S(1)}, u32[]{:S(2)}, u32[]{:S(2)}) collective-permute-start(f32[72,1,128]{2,1,0:T(1,128)S(1)} %get-tuple-element.104), channel_id=1, source_target_pairs={{4,0},{8,4},{12,8},{5,1},{9,5},{13,9},{6,2},{10,6},{14,10},{7,3},{... | collective-permute-start | bytes 110600 | tf_op jit(solution)/shard_map/ppermute | solution.py:23
  136.1 16.4 %collective-permute-start.22 = (bf16[5,1,16,2048]{3,2,1,0:T(8,128)(2,1)}, bf16[5,1,16,2048]{3,2,1,0:T(8,128)(2,1)}, u32[]{:S(2)}, u32[]{:S(2)}) collective-permute-start(bf16[5,1,16,2048]{3,2,1,0:T(8,128)(2,1)} %get-tuple-element.83), channel_id=1, source_target_pairs={{0,1},{1,2},{2,3},{4,5},{5,6},{6,7},{8,9},{9,10},{10,11},{12,13},{... | collective-permute-start | bytes 983048 | tf_op jit(solution)/shard_map/ppermute | solution.py:20
  138.2 14.3 %collective-permute-start.23 = (bf16[5,1,16,2048]{3,2,1,0:T(8,128)(2,1)}, bf16[5,1,16,2048]{3,2,1,0:T(8,128)(2,1)}, u32[]{:S(2)}, u32[]{:S(2)}) collective-permute-start(bf16[5,1,16,2048]{3,2,1,0:T(8,128)(2,1)} %get-tuple-element.84), channel_id=1, source_target_pairs={{1,0},{2,1},{3,2},{5,4},{6,5},{7,6},{9,8},{10,9},{11,10},{13,12},{... | collective-permute-start | bytes 983048 | tf_op jit(solution)/shard_map/ppermute | solution.py:23
  147.5 19.8 %collective-permute-start.15 = (f32[72,18,1]{0,2,1:T(1,128)}, f32[72,18,1]{0,2,1:T(1,128)}, u32[]{:S(2)}, u32[]{:S(2)}) collective-permute-start(f32[72,18,1]{0,2,1:T(1,128)} %copy.92), channel_id=1, source_target_pairs={{0,1},{1,2},{2,3},{4,5},{5,6},{6,7},{8,9},{9,10},{10,11},{12,13},{... | collective-permute-start | bytes 15560 | tf_op jit(solution)/shard_map/ppermute | solution.py:20
  150.2 16.0 %collective-permute-start.14 = (f32[72,18,1]{0,2,1:T(1,128)}, f32[72,18,1]{0,2,1:T(1,128)}, u32[]{:S(2)}, u32[]{:S(2)}) collective-permute-start(f32[72,18,1]{0,2,1:T(1,128)} %copy.90), channel_id=1, source_target_pairs={{1,0},{2,1},{3,2},{5,4},{6,5},{7,6},{9,8},{10,9},{11,10},{13,12},{... | collective-permute-start | bytes 15560 | tf_op jit(solution)/shard_map/ppermute | solution.py:23
  159.7 9.6 %collective-permute-start.25 = (f32[60,1,256]{2,0,1:T(8,128)}, f32[60,1,256]{2,0,1:T(8,128)S(1)}, u32[]{:S(2)}, u32[]{:S(2)}) collective-permute-start(f32[60,1,256]{2,0,1:T(8,128)} %get-tuple-element.79), channel_id=1, source_target_pairs={{0,4},{4,8},{8,12},{1,5},{5,9},{9,13},{2,6},{6,10},{10,14},{3,7},{... | collective-permute-start | bytes 184328 | tf_op jit(solution)/shard_map/ppermute | solution.py:20
  164.0 6.0 %collective-permute-start.24 = (f32[60,1,256]{2,0,1:T(8,128)S(1)}, f32[60,1,256]{2,0,1:T(8,128)S(1)}, u32[]{:S(2)}, u32[]{:S(2)}) collective-permute-start(f32[60,1,256]{2,0,1:T(8,128)S(1)} %get-tuple-element.80), channel_id=1, source_target_pairs={{4,0},{8,4},{12,8},{5,1},{9,5},{13,9},{6,2},{10,6},{14,10},{7,3},{... | collective-permute-start | bytes 184328 | tf_op jit(solution)/shard_map/ppermute | solution.py:23
  175.1 11.0 %collective-permute-start.27 = (f32[60,18,1]{0,2,1:T(1,128)S(1)}, f32[60,18,1]{0,2,1:T(1,128)}, u32[]{:S(2)}, u32[]{:S(2)}) collective-permute-start(f32[60,18,1]{0,2,1:T(1,128)S(1)} %copy.111), channel_id=1, source_target_pairs={{0,1},{1,2},{2,3},{4,5},{5,6},{6,7},{8,9},{9,10},{10,11},{12,13},{... | collective-permute-start | bytes 12968 | tf_op jit(solution)/shard_map/ppermute | solution.py:20
  178.9 5.3 %collective-permute-start.26 = (f32[60,18,1]{0,2,1:T(1,128)}, f32[60,18,1]{0,2,1:T(1,128)}, u32[]{:S(2)}, u32[]{:S(2)}) collective-permute-start(f32[60,18,1]{0,2,1:T(1,128)} %copy.109), channel_id=1, source_target_pairs={{1,0},{2,1},{3,2},{5,4},{6,5},{7,6},{9,8},{10,9},{11,10},{13,12},{... | collective-permute-start | bytes 12968 | tf_op jit(solution)/shard_map/ppermute | solution.py:23
  191.1 6.0 %collective-permute-start.29 = (f32[60,1,256]{2,0,1:T(8,128)S(1)}, f32[60,1,256]{2,0,1:T(8,128)S(1)}, u32[]{:S(2)}, u32[]{:S(2)}) collective-permute-start(f32[60,1,256]{2,0,1:T(8,128)S(1)} %get-tuple-element.77), channel_id=1, source_target_pairs={{0,4},{4,8},{8,12},{1,5},{5,9},{9,13},{2,6},{6,10},{10,14},{3,7},{... | collective-permute-start | bytes 184328 | tf_op jit(solution)/shard_map/ppermute | solution.py:20
  194.8 5.0 %collective-permute-start.28 = (f32[60,1,256]{2,0,1:T(8,128)S(1)}, f32[60,1,256]{2,0,1:T(8,128)S(1)}, u32[]{:S(2)}, u32[]{:S(2)}) collective-permute-start(f32[60,1,256]{2,0,1:T(8,128)S(1)} %get-tuple-element.78), channel_id=1, source_target_pairs={{4,0},{8,4},{12,8},{5,1},{9,5},{13,9},{6,2},{10,6},{14,10},{7,3},{... | collective-permute-start | bytes 184328 | tf_op jit(solution)/shard_map/ppermute | solution.py:23
  203.7 9.9 %collective-permute-start.31 = (f32[60,18,1]{0,2,1:T(1,128)S(1)}, f32[60,18,1]{0,2,1:T(1,128)S(1)}, u32[]{:S(2)}, u32[]{:S(2)}) collective-permute-start(f32[60,18,1]{0,2,1:T(1,128)S(1)} %copy.115), channel_id=1, source_target_pairs={{0,1},{1,2},{2,3},{4,5},{5,6},{6,7},{8,9},{9,10},{10,11},{12,13},{... | collective-permute-start | bytes 12968 | tf_op jit(solution)/shard_map/ppermute | solution.py:20
  219.5 5.2 %collective-permute-start.33 = (f32[60,1,256]{2,0,1:T(8,128)S(1)}, f32[60,1,256]{2,0,1:T(8,128)S(1)}, u32[]{:S(2)}, u32[]{:S(2)}) collective-permute-start(f32[60,1,256]{2,0,1:T(8,128)S(1)} %get-tuple-element.75), channel_id=1, source_target_pairs={{0,4},{4,8},{8,12},{1,5},{5,9},{9,13},{2,6},{6,10},{10,14},{3,7},{... | collective-permute-start | bytes 184328 | tf_op jit(solution)/shard_map/ppermute | solution.py:20
  222.7 5.0 %collective-permute-start.32 = (f32[60,1,256]{2,0,1:T(8,128)S(1)}, f32[60,1,256]{2,0,1:T(8,128)S(1)}, u32[]{:S(2)}, u32[]{:S(2)}) collective-permute-start(f32[60,1,256]{2,0,1:T(8,128)S(1)} %get-tuple-element.76), channel_id=1, source_target_pairs={{4,0},{8,4},{12,8},{5,1},{9,5},{13,9},{6,2},{10,6},{14,10},{7,3},{... | collective-permute-start | bytes 184328 | tf_op jit(solution)/shard_map/ppermute | solution.py:23
  229.2 8.8 %collective-permute-start.35 = (f32[60,18,1]{0,2,1:T(1,128)S(1)}, f32[60,18,1]{0,2,1:T(1,128)S(1)}, u32[]{:S(2)}, u32[]{:S(2)}) collective-permute-start(f32[60,18,1]{0,2,1:T(1,128)S(1)} %copy.119), channel_id=1, source_target_pairs={{0,1},{1,2},{2,3},{4,5},{5,6},{6,7},{8,9},{9,10},{10,11},{12,13},{... | collective-permute-start | bytes 12968 | tf_op jit(solution)/shard_map/ppermute | solution.py:20
  (46 other events, 316.6 us)
where the time goes:
time: 245 us; the launch traced here: 243 us
  starting transfers between devices  92.9 us (38%)
  local copies, waits for them, and re-layouts  66.1 us (27%)
  matrix products  29.1 us (12%)
  blocking collectives  21 us (9%)
  waiting for transfers between devices  17.9 us (7%)
  other arithmetic  13.8 us (6%)
    ppermute x18, starting transfers between devices, extended(): lax.ppermute(lax.slice_in_dim(block, block.shape[dim] - width, None, axis...  61.4 us
    ppermute x18, starting transfers between devices, extended(): lax.ppermute(lax.slice_in_dim(block, 0, width, axis=dim), axis, backward)  31.5 us
    all_gather x1, blocking collectives, body(): every_row = lax.all_gather(surface, ('comp', 'lev'), axis=0, tiled=True)  21 us
    slice x17, local copies, waits for them, and re-layouts, extended(): lax.slice_in_dim(block, 0, width, axis=dim)  20.1 us
    ppermute x18, waiting for transfers between devices, extended(): lax.ppermute(lax.slice_in_dim(block, 0, width, axis=dim), axis, backward)  17.9 us
    dot_general x8, matrix products, column_mix(): jnp.einsum('kj,jyx->kyx', matrix, field, precision=lax.Precision.HIGHEST)  16.7 us
    slice x16, local copies, waits for them, and re-layouts, extended(): lax.slice_in_dim(block, block.shape[dim] - width, None, axis=dim)  12.2 us
    unnamed x94, local copies, waits for them, and re-layouts  12.1 us
  transfers between devices with their start and end apart: 36, of which 9 were waited for; matrix products, arithmetic and copies ran while one was open for 30% of the time, Pallas kernels for 0%

commit v1 on v0

v1 whole, which is shorter than its diff:
```python
import jax
import jax.numpy as jnp
from jax import lax
from jax.experimental import pallas as pl
from jax.experimental.pallas import tpu as pltpu
from jax.sharding import PartitionSpec as P

STEPS = 4
RATE = 0.24
LINK = 0.5
BF16 = jnp.bfloat16
F32 = jnp.float32
MESH = pl.DeviceIdType.MESH
NEAR = [(n // 3 - 1, n % 3 - 1) for n in range(9)]
SIDES = [(-1, 0), (1, 0), (0, -1), (0, 1)]


def halves(x):
    hi = x.astype(BF16)
    return hi, (x - hi.astype(F32)).astype(BF16)


def split_outside(x):
    hi = lax.reduce_precision(x, 8, 7)
    return hi.astype(BF16), (x - hi).astype(BF16)


def padded(x, rows, cols):
    return jnp.pad(x, ((0, rows - x.shape[0]), (0, cols - x.shape[1])))


def reflect(index, count):
    return jnp.where(
        index < 0, -index, jnp.where(index > count - 1, 2 * (count - 1) - index, index)
    )


def make_kernel(dims):
    rows, per_tile, chan, cells_a, cells_o, last, counts = dims
    pairs = rows * per_tile

    def kernel(
        ocean_in, atm_in, flux_ref, weight_in, surf_in, slot_row, slot_col, omat, amat, coef, wet,
        ocean_out, atm_out, flux_out,
        ocean, atm, wbuf, prod, part, precv, surf, gathered, forced, ou, au, sst,
        orow, ocol, oedge, arow, acol, aedge,
        in_sem, w_sem, surf_send, surf_recv, part_send, part_recv,
        o_send, o_recv, a_send, a_recv,
    ):
        ci = lax.axis_index("comp")
        li = lax.axis_index("lev")
        comp_count, lev_count = counts

        def there(di, dj):
            ok = None
            for delta, index, count in ((di, ci, comp_count), (dj, li, lev_count)):
                if delta == -1:
                    one = index > 0
                elif delta == 1:
                    one = index < count - 1
                else:
                    continue
                ok = one if ok is None else jnp.logical_and(ok, one)
            return ok

        def device(di, dj):
            return {
                "comp": jnp.clip(ci + di, 0, comp_count - 1),
                "lev": jnp.clip(li + dj, 0, lev_count - 1),
            }

        load_ocean = pltpu.make_async_copy(ocean_in, ocean, in_sem.at[0])
        load_atm = pltpu.make_async_copy(atm_in, atm, in_sem.at[1])
        load_ocean.start()
        load_atm.start()

        def load_weight(y):
            return pltpu.make_async_copy(weight_in.at[y], wbuf.at[y], w_sem.at[y])

        def start_weight(y, carry):
            load_weight(y).start()
            return carry

        lax.fori_loop(0, rows, start_weight, 0)

        surf[4] = surf_in[...]
        for n, (di, dj) in enumerate(NEAR):
            if n != 4:
                @pl.when(jnp.logical_not(there(di, dj)))
                def _():
                    surf[n] = jnp.zeros_like(surf_in)
        for side, (di, dj) in enumerate(SIDES):
            @pl.when(jnp.logical_not(there(di, dj)))
            def _():
                for rbuf, cbuf in ((orow, ocol), (arow, acol)):
                    buf = rbuf if side < 2 else cbuf
                    for s in range(STEPS):
                        buf[s, side % 2] = jnp.zeros(buf.shape[2:], F32)

        barrier = pltpu.get_barrier_semaphore()
        for n, (di, dj) in enumerate(NEAR):
            if n != 4:
                @pl.when(there(di, dj))
                def _():
                    pl.semaphore_signal(
                        barrier, inc=1, device_id=device(di, dj), device_id_type=MESH
                    )
        tall = 1 + (ci > 0).astype(jnp.int32) + (ci < comp_count - 1).astype(jnp.int32)
        wide = 1 + (li > 0).astype(jnp.int32) + (li < lev_count - 1).astype(jnp.int32)

        def remote(src, dst, send, recv, di, dj):
            return pltpu.make_async_remote_copy(
                src_ref=src, dst_ref=dst, send_sem=send, recv_sem=recv,
                device_id=device(di, dj), device_id_type=MESH,
            )

        def surf_copy(n):
            return remote(
                surf.at[4], surf.at[8 - n], surf_send.at[n], surf_recv.at[n], *NEAR[n]
            )

        def part_copy(n):
            return remote(
                part.at[n], precv.at[n], part_send.at[n], part_recv.at[n], *NEAR[n]
            )

        def side_copy(state, rbuf, cbuf, edge, send, recv, s, side):
            if side < 2:
                src = state.at[0 if side == 0 else rows - 1]
                dst = rbuf.at[s, 1 - side]
            else:
                src = edge.at[side - 2]
                dst = cbuf.at[s, 3 - side]
            return remote(
                src, dst, send.at[s, side], recv.at[s, side], *SIDES[side]
            )

        ocean_parts = (ocean, orow, ocol, oedge, o_send, o_recv)
        atm_parts = (atm, arow, acol, aedge, a_send, a_recv)

        def start_sides(parts, s):
            for side, (di, dj) in enumerate(SIDES):
                @pl.when(there(di, dj))
                def _():
                    side_copy(*parts, s, side).start()

        def wait_sent(parts, s):
            for side, (di, dj) in enumerate(SIDES):
                @pl.when(there(di, dj))
                def _():
                    side_copy(*parts, s, side).wait_send()

        def wait_sides(parts, s):
            for side, (di, dj) in enumerate(SIDES):
                @pl.when(there(-di, -dj))
                def _():
                    side_copy(*parts, s, side).wait_recv()

        def pack(slabs, edge):
            depth = edge.shape[1]
            lane = lax.broadcasted_iota(jnp.int32, (depth, 128), 1)
            left = jnp.zeros((depth, 128), F32)
            right = jnp.zeros((depth, 128), F32)
            for r in range(rows):
                first, final = slabs(r)
                left = jnp.where(lane == r, pltpu.roll(first, r, 1) if r else first, left)
                right = jnp.where(lane == r, pltpu.roll(final, r + 1, 1), right)
            edge[0] = left
            edge[1] = right

        def ends(state):
            width = state.shape[2]
            return lambda r: (state[r, :, 0:128], state[r, :, width - 128:width])

        load_ocean.wait()
        pack(ends(ocean), oedge)
        load_atm.wait()
        pack(ends(atm), aedge)
        pl.semaphore_wait(barrier, tall * wide - 1)

        for n, (di, dj) in enumerate(NEAR):
            if n != 4:
                @pl.when(there(di, dj))
                def _():
                    surf_copy(n).start()
        start_sides(atm_parts, 0)
        start_sides(ocean_parts, 0)

        which = lax.broadcasted_iota(jnp.int32, (chan * per_tile, cells_a), 0) % per_tile

        def multiply(y, carry):
            load_weight(y).wait()
            flux = flux_ref[y]
            left = jnp.concatenate(
                [jnp.where(which == p, flux, 0.0).astype(BF16) for p in range(per_tile)], axis=1
            )
            out = jnp.dot(left, wbuf[y], preferred_element_type=F32)
            at = pl.ds(pl.multiple_of(y * per_tile, per_tile), per_tile)
            for c in range(chan):
                prod[c, at, :] = out[c * per_tile:(c + 1) * per_tile]
            return carry

        lax.fori_loop(0, rows, multiply, 0)

        slots = 9 * rows
        pick = (
            lax.broadcasted_iota(jnp.int32, (slots, pairs), 0) == slot_row[...]
        ).astype(F32).astype(BF16)
        pick = jnp.concatenate([pick, pick], axis=1)
        for c in range(chan):
            hi, lo = halves(prod[c])
            sums = jnp.dot(
                pick, jnp.concatenate([hi, lo], axis=0), preferred_element_type=F32
            ).astype(BF16)
            for n in range(9):
                part[n, c] = sums[n * rows:(n + 1) * rows]
        for n, (di, dj) in enumerate(NEAR):
            if n != 4:
                @pl.when(there(di, dj))
                def _():
                    part_copy(n).start()

        for n, (di, dj) in enumerate(NEAR):
            if n != 4:
                @pl.when(there(-di, -dj))
                def _():
                    surf_copy(n).wait_recv()
        group = 16
        wanted = (
            lax.broadcasted_iota(jnp.int32, (rows * group, slots), 1) == slot_col[...]
        ).astype(F32).astype(BF16)
        found = jnp.dot(wanted, surf[...].reshape(slots, cells_o), preferred_element_type=F32)
        spare = lax.broadcasted_iota(jnp.int32, (rows * group, cells_o), 0) % group >= per_tile
        gathered[...] = jnp.where(spare, 1.0, found).astype(BF16).reshape(rows, group, cells_o)
        line = lax.broadcasted_iota(jnp.int32, (8, cells_a), 0)

        def regrid(y, carry):
            out = lax.dot_general(
                gathered[y], wbuf[y], (((1,), (1,)), ((), ())), preferred_element_type=F32
            )
            num = jnp.zeros((8, cells_a), F32)
            den = jnp.zeros((8, cells_a), F32)
            for p in range(per_tile):
                cols = slice(p * cells_a, (p + 1) * cells_a)
                num = num + jnp.where(line == p, out[0:8, cols], 0.0)
                den = den + out[8:16, cols]
            total = jnp.sum(num, axis=0, keepdims=True)
            sst[y] = jnp.broadcast_to(total, (8, cells_a)) / den
            return carry

        lax.fori_loop(0, rows, regrid, 0)
        flux_out[...] = jnp.zeros_like(flux_out)

        def stencil(parts, s, r):
            state, rbuf, cbuf = parts[0], parts[1], parts[2]
            depth, width = state.shape[1], state.shape[2]
            lane = lax.broadcasted_iota(jnp.int32, (depth, 128), 1)
            x = state[r]
            up = rbuf[s, 0] if r == 0 else state[r - 1]
            down = rbuf[s, 1] if r == rows - 1 else state[r + 1]
            west = pltpu.roll(x, 1, 1)
            east = pltpu.roll(x, width - 1, 1)
            from_west = cbuf[s, 0]
            if r:
                from_west = pltpu.roll(from_west, 128 - r, 1)
            from_east = pltpu.roll(cbuf[s, 1], 127 - r, 1)
            west_end = jnp.where(lane == 0, from_west, west[:, 0:128])
            east_end = jnp.where(lane == 127, from_east, east[:, width - 128:width])
            if width > 128:
                west_end = jnp.concatenate([west_end, west[:, 128:]], axis=1)
                east_end = jnp.concatenate([east[:, 0:width - 128], east_end], axis=1)
            return (1.0 - 4.0 * RATE) * x + RATE * ((up + down) + (west_end + east_end))

        def step(s, carry):
            wait_sides(atm_parts, s)
            for r in range(rows):
                hi, lo = halves(stencil(atm_parts, s, r))
                au[r] = jnp.concatenate([hi, hi, lo], axis=0)
            wait_sent(atm_parts, s)
            depth = atm.shape[1]
            level = lax.broadcasted_iota(jnp.int32, (depth, cells_a), 0)
            for r in range(rows):
                mixed = jnp.dot(amat[...], au[r], preferred_element_type=F32)
                gap = sst[r, 0:1] - mixed[last:last + 1]
                flux_out[r] += mixed[last + 1:last + 1 + chan] + coef[...] * gap
                atm[r] = mixed + jnp.where(level == last, LINK * gap, 0.0)

            @pl.when(s < STEPS - 1)
            def _():
                pack(ends(atm), aedge)
                start_sides(atm_parts, s + 1)

            @pl.when(s == 0)
            def _():
                total = part[4].astype(F32).reshape(chan * rows, cells_o)
                prod[0, 0:chan * rows] = total
                for n, (di, dj) in enumerate(NEAR):
                    if n != 4:
                        @pl.when(there(-di, -dj))
                        def _():
                            part_copy(n).wait_recv()
                            prod[0, 0:chan * rows] += precv[n].astype(F32).reshape(
                                chan * rows, cells_o
                            )
                size = 4 * chan
                to = lax.broadcasted_iota(jnp.int32, (rows * size, chan * rows), 0)
                source = lax.broadcasted_iota(jnp.int32, (rows * size, chan * rows), 1)
                place = to % size
                turn = (
                    jnp.logical_and(
                        source == (place % chan) * rows + to // size, place < 3 * chan
                    )
                ).astype(F32).astype(BF16)
                hi, lo = halves(prod[0, 0:chan * rows])
                laid = jnp.dot(
                    jnp.concatenate([turn, turn], axis=1),
                    jnp.concatenate([hi, lo], axis=0),
                    preferred_element_type=F32,
                )
                high = laid.astype(BF16).astype(F32)
                at = lax.broadcasted_iota(jnp.int32, laid.shape, 0) % size
                both = jnp.where(at < 2 * chan, high, laid - high).astype(BF16)
                both = both.reshape(rows, size, cells_o)
                mixing = 3 * ocean.shape[1]
                for r in range(rows):
                    ou[r, mixing:mixing + size] = both[r]

            wait_sides(ocean_parts, s)
            deep = ocean.shape[1]
            for r in range(rows):
                hi, lo = halves(stencil(ocean_parts, s, r))
                ou[r, 0:3 * deep] = jnp.concatenate([hi, hi, lo], axis=0)
            wait_sent(ocean_parts, s)
            for r in range(rows):
                ocean[r] = wet[r:r + 1] * jnp.dot(
                    omat[...], ou[r], preferred_element_type=F32
                )

            @pl.when(s < STEPS - 1)
            def _():
                pack(ends(ocean), oedge)
                start_sides(ocean_parts, s + 1)

            return carry

        lax.fori_loop(0, STEPS, step, 0)

        save_ocean = pltpu.make_async_copy(ocean, ocean_out, in_sem.at[0])
        save_atm = pltpu.make_async_copy(atm, atm_out, in_sem.at[1])
        save_ocean.start()
        save_atm.start()
        for n, (di, dj) in enumerate(NEAR):
            if n != 4:
                @pl.when(there(di, dj))
                def _():
                    surf_copy(n).wait_send()
                    part_copy(n).wait_send()
        save_ocean.wait()
        save_atm.wait()

    return kernel


def body(
    atm_state,
    ocean_state,
    flux_prev,
    pair_offset,
    pair_tile,
    pair_weight,
    atm_mix,
    ocean_mix,
    exchange_response_matrix,
    exchange_factor_array,
    depth_profile,
    sea_mask,
):
    comp_count = lax.axis_size("comp")
    lev_count = lax.axis_size("lev")
    row_block = lax.axis_index("comp")
    col_block = lax.axis_index("lev")
    pairs, cells_a, cells_o = pair_weight.shape
    air, rows = atm_state.shape[:2]
    sea = ocean_state.shape[0]
    chan = flux_prev.shape[0]
    per_tile = pairs // rows
    deep = (sea + 15) // 16 * 16
    high = (air + chan + 15) // 16 * 16

    dest_row = reflect(row_block + pair_offset // 3 - 1, comp_count)
    dest_col = reflect(col_block + pair_offset % 3 - 1, lev_count)
    slot = ((dest_row - row_block + 1) * 3 + (dest_col - col_block + 1)) * rows + pair_tile
    slot_col = jnp.pad(
        slot.reshape(rows, per_tile), ((0, 0), (0, 16 - per_tile)), constant_values=-1
    ).reshape(rows * 16, 1)

    ocean_t = jnp.pad(ocean_state.transpose(1, 0, 2), ((0, 0), (0, deep - sea), (0, 0)))
    atm_t = jnp.pad(atm_state.transpose(1, 0, 2), ((0, 0), (0, high - air), (0, 0)))
    flux_t = jnp.repeat(flux_prev.transpose(1, 0, 2), per_tile, axis=1)
    surface = ocean_state[0].astype(BF16)

    omix_hi, omix_lo = split_outside(padded(ocean_mix, deep, deep))
    depth_hi, depth_lo = split_outside(padded(depth_profile, deep, chan))
    omat = jnp.concatenate(
        [omix_hi, omix_lo, omix_hi, depth_hi, depth_lo, depth_hi, jnp.zeros_like(depth_hi)], axis=1
    )
    response = jnp.dot(exchange_response_matrix, atm_mix, precision=lax.Precision.HIGHEST)
    amix_hi, amix_lo = split_outside(
        padded(jnp.concatenate([atm_mix, response], axis=0), high, high)
    )
    amat = jnp.concatenate([amix_hi, amix_lo, amix_hi], axis=1)
    coef = jnp.broadcast_to(
        (exchange_factor_array + LINK * exchange_response_matrix[:, air - 1])[:, None],
        (chan, cells_a),
    )
    dims = (rows, per_tile, chan, cells_a, cells_o, air - 1, (comp_count, lev_count))
    anywhere = pl.BlockSpec(memory_space=pl.ANY)
    vmem = pl.BlockSpec(memory_space=pltpu.VMEM)
    dma = pltpu.SemaphoreType.DMA
    ocean_end, atm_end, flux_end = pl.pallas_call(
        make_kernel(dims),
        out_shape=(
            jax.ShapeDtypeStruct((rows, deep, cells_o), F32),
            jax.ShapeDtypeStruct((rows, high, cells_a), F32),
            jax.ShapeDtypeStruct((rows, chan, cells_a), F32),
        ),
        in_specs=[anywhere, anywhere, vmem, anywhere] + [vmem] * 7,
        out_specs=(anywhere, anywhere, vmem),
        scratch_shapes=[
            pltpu.VMEM((rows, deep, cells_o), F32),
            pltpu.VMEM((rows, high, cells_a), F32),
            pltpu.VMEM((rows, per_tile * cells_a, cells_o), BF16),
            pltpu.VMEM((chan, pairs, cells_o), F32),
            pltpu.VMEM((9, chan, rows, cells_o), BF16),
            pltpu.VMEM((9, chan, rows, cells_o), BF16),
            pltpu.VMEM((9, rows, cells_o), BF16),
            pltpu.VMEM((rows, 16, cells_o), BF16),
            pltpu.VMEM((8, 128), F32),
            pltpu.VMEM((rows, 3 * deep + 4 * chan, cells_o), BF16),
            pltpu.VMEM((rows, 3 * high, cells_a), BF16),
            pltpu.VMEM((rows, 8, cells_a), F32),
            pltpu.VMEM((STEPS, 2, deep, cells_o), F32),
            pltpu.VMEM((STEPS, 2, deep, 128), F32),
            pltpu.VMEM((2, deep, 128), F32),
            pltpu.VMEM((STEPS, 2, high, cells_a), F32),
            pltpu.VMEM((STEPS, 2, high, 128), F32),
            pltpu.VMEM((2, high, 128), F32),
            dma((2,)),
            dma((rows,)),
            dma((9,)),
            dma((9,)),
            dma((9,)),
            dma((9,)),
            dma((STEPS, 4)),
            dma((STEPS, 4)),
            dma((STEPS, 4)),
            dma((STEPS, 4)),
        ],
        compiler_params=pltpu.CompilerParams(
            collective_id=0, has_side_effects=True, vmem_limit_bytes=40 * 1024 * 1024
        ),
        name="coupled",
    )(
        ocean_t, atm_t, flux_t,
        pair_weight.reshape(rows, per_tile * cells_a, cells_o),
        surface, slot.reshape(1, pairs), slot_col, omat, amat, coef, sea_mask.astype(F32),
    )
    return (
        atm_end[:, :air].transpose(1, 0, 2),
        ocean_end[:, :sea].transpose(1, 0, 2),
        (flux_end / STEPS).transpose(1, 0, 2).astype(BF16),
    )


def solution(mesh):
    in_specs = (
        P("member", "comp", "lev"),
        P("member", "comp", "lev"),
        P("member", "comp", "lev"),
        P(("comp", "lev")),
        P(("comp", "lev")),
        P(("comp", "lev"), None, None),
        P(),
        P(),
        P(),
        P(),
        P(),
        P("comp", "lev"),
    )
    out_specs = (P("member", "comp", "lev"), P("member", "comp", "lev"), P("member", "comp", "lev"))
    return jax.shard_map(body, mesh=mesh, in_specs=in_specs, out_specs=out_specs, check_vma=False)
```

time: 245 us -> 53.1 us (0.22)
  the two profiles are of different devices: /device:TPU:1 before, /device:TPU:0 now
where the time goes in v1:
time: 53.1 us; the launch traced here: 52.4 us
  Pallas kernels  33.7 us (63%)
  local copies, waits for them, and re-layouts  12.4 us (23%)
  other arithmetic  4.61 us (9%)
  matrix products  0.92 us (2%)
  between operations  0.75 us (1%)
    pallas_call x1, Pallas kernels, body(): pl.pallas_call(make_kernel(dims), out_shape=(jax.ShapeDtypeStruct((rows,...  33.7 us
    unnamed x8, local copies, waits for them, and re-layouts  10.3 us
    convert_element_type x3, other arithmetic, split_outside(): return (hi.astype(BF16), (x - hi).astype(BF16))  1.57 us

profile of v1, /device:TPU:0, one launch (start us, length us, event | category | flops | bytes accessed | tf_op | source)
XLA Modules:
  0.0 52.4 jit_solution(6912318485308809047)
XLA Ops:
  0.6 0.7 %multiply_add_fusion = s32[128]{0:T(128)S(1)} fusion(s32[128]{0:T(128)} %param.16, s32[128]{0:T(128)} %param.15, s32[]{:T(128)S(6)} %axis_index.25, s32[]{:T(128)S(6)} %axis_index.23), kind=kLoop, calls=%fused_computation.30 | loop fusion | flops 4608 | bytes 1544 | tf_op jit(solution)/shard_map/add | solution.py:392
  1.3 0.9 %multiply_reduce_fusion = f32[8]{0:T(128)S(1)} fusion(f32[8,72]{1,0:T(8,128)} %param.20), kind=kLoop, calls=%fused_computation.21 | loop fusion | flops 8 | bytes 64 | tf_op jit(solution)/shard_map/mul | solution.py:413
  2.2 0.7 %add.57 = f32[8]{0:T(128)S(1)} add(f32[8]{0:T(128)} %param.21, f32[8]{0:T(128)S(1)} %multiply_reduce_fusion) | non-fusion elementwise | flops 8 | bytes 96 | tf_op jit(solution)/shard_map/add | solution.py:413
  2.9 0.1 broadcast_in_dim.14.coef
  2.9 0.9 %fusion.7 = f32[8,72]{1,0:T(8,128)S(1)} fusion(f32[8,72]{1,0:T(8,128)} %param.20, f32[72,72]{1,0:T(8,128)} %param.18), kind=kOutput, calls=%fused_computation.31 | convolution fusion | flops 497664 | bytes 25344 | tf_op jit(solution)/shard_map/dot_general | solution.py:407
  3.9 0.1 reshape.28
  4.0 0.7 %fusion.4.surf_in = bf16[16,256]{1,0:T(8,128)(2,1)S(1)} fusion(f32[60,16,256]{2,1,0:T(8,128)} %param.13), kind=kLoop, calls=%fused_computation.20 | loop fusion | bytes 16384 | tf_op jit(solution)/shard_map/convert_element_type | solution.py:400
  4.7 0.7 %convert_element_type.47.wet = f32[16,256]{1,0:T(8,128)S(1)} convert(s32[16,256]{1,0:T(8,128)} %param.23) | non-fusion elementwise | flops 4096 | bytes 32768 | tf_op jit(solution)/shard_map/convert_element_type | solution.py:466
  5.4 0.8 %copy.32 = bf16[16,8,128]{2,1,0:T(8,128)(2,1)S(1)} copy(bf16[16,8,128]{2,0,1:T(8,128)(2,1)} %bitcast.25) | data formatting | bytes 65536 | tf_op jit(solution)/shard_map/transpose | solution.py:399
  6.2 0.8 %copy.33 = f32[60,8]{1,0:T(8,128)S(1)} copy(f32[60,8]{0,1:T(8,128)} %param.22) | data formatting | bytes 3840 | tf_op args[10]
  7.0 0.8 %fusion.1 = (bf16[64,64]{1,0:T(8,128)(2,1)S(1)}, bf16[64,64]{1,0:T(8,128)(2,1)S(1)}) fusion(f32[60,60]{1,0:T(8,128)} %param.19), kind=kLoop, calls=%fused_computation.16 | loop fusion | flops 16384 | bytes 30784 | tf_op jit(solution)/shard_map/convert_element_type | solution.py:25
  7.8 0.1 concatenate.9.omat
  7.9 0.8 %fusion = (bf16[80,80]{1,0:T(8,128)(2,1)S(1)}, bf16[80,80]{1,0:T(8,128)(2,1)S(1)}) fusion(f32[8,72]{1,0:T(8,128)S(1)} %fusion.7, f32[72,72]{1,0:T(8,128)} %param.18), kind=kLoop, calls=%fused_computation.12 | loop fusion | flops 51200 | bytes 48640 | tf_op jit(solution)/shard_map/convert_element_type | solution.py:25
  8.7 0.1 pad_maximum_fusion.amat
  8.8 0.1 reshape.30.slot_col
  8.9 1.3 %copy.41 = f32[72,16,128]{2,0,1:T(8,128)S(1)} copy(f32[72,16,128]{2,1,0:T(8,128)} %param.12) | data formatting | bytes 1179648 | tf_op args[0]
  10.2 1.8 %copy.40 = f32[60,16,256]{2,0,1:T(8,128)S(1)} copy(f32[60,16,256]{2,1,0:T(8,128)} %param.13) | data formatting | bytes 1966080 | tf_op args[1]
  12.0 0.1 pad.24.ocean_in
  12.1 0.0 copy-start
  12.1 3.4 %copy-done = bf16[128,128,256]{2,1,0:T(8,128)(2,1)S(1)} copy-done((bf16[128,128,256]{2,1,0:T(8,128)(2,1)S(1)}, bf16[128,128,256]{2,1,0:T(8,128)(2,1)}, u32[]{:S(2)}) %copy-start) | copy-done | bytes 8388632
  15.5 33.7 %coupled.1 = (f32[16,64,256]{2,1,0:T(8,128)S(1)}, f32[16,80,128]{2,1,0:T(8,128)S(1)}, f32[16,8,128]{2,1,0:T(8,128)S(1)}) custom-call(f32[16,64,256]{2,1,0:T(8,128)S(1)} %pad.24.ocean_in, f32[16,80,128]{2,1,0:T(8,128)S(1)} %pad.25.atm_in, bf16[16,64,128]{2,1,0:T(8,128)(2,1)S(1)} %broadcast_bitcast_fusion.flux_ref, bf16[16,1024,256]{2,1,0:T(8,128)(2,1)S(1)} %bitcast.21, ...), custom_call_target="tpu_custom_call" | custom-call | tf_op jit(solution)/shard_map/coupled/pallas_call | solution.py:420
  49.2 0.9 %copy.35 = f32[72,16,128]{2,1,0:T(8,128)} copy(f32[72,16,128]{2,0,1:T(8,128)S(1)} %slice_bitcast_fusion.1) | data formatting | bytes 1179648
  50.2 0.6 %copy.37 = bf16[8,16,128]{2,1,0:T(8,128)(2,1)} copy(bf16[8,16,128]{2,0,1:T(8,128)(2,1)S(1)} %fusion.3) | data formatting | bytes 65536
  50.8 0.1 slice_bitcast_fusion
  50.9 1.5 %copy.36 = f32[60,16,256]{2,1,0:T(8,128)} copy(f32[60,16,256]{2,0,1:T(8,128)S(1)} %slice_bitcast_fusion) | data formatting | bytes 1966080
  (7 shorter events, 0.2 us)
Async XLA Ops:
  12.1 3.4 %copy-start = (bf16[128,128,256]{2,1,0:T(8,128)(2,1)S(1)}, bf16[128,128,256]{2,1,0:T(8,128)(2,1)}, u32[]{:S(2)}) copy-start(bf16[128,128,256]{2,1,0:T(8,128)(2,1)} %param.17) | copy-start | bytes 25165828

commit v2 on v1

--- a/solution.py
+++ b/solution.py
@@ -20,15 +20,6 @@
     return hi, (x - hi.astype(F32)).astype(BF16)
 
 
-def split_outside(x):
-    hi = lax.reduce_precision(x, 8, 7)
-    return hi.astype(BF16), (x - hi).astype(BF16)
-
-
-def padded(x, rows, cols):
-    return jnp.pad(x, ((0, rows - x.shape[0]), (0, cols - x.shape[1])))
-
-
 def reflect(index, count):
     return jnp.where(
         index < 0, -index, jnp.where(index > count - 1, 2 * (count - 1) - index, index)
@@ -36,15 +27,17 @@
 
 
 def make_kernel(dims):
-    rows, per_tile, chan, cells_a, cells_o, last, counts = dims
+    rows, per_tile, chan, cells_a, cells_o, last, sea_levels, counts = dims
     pairs = rows * per_tile
 
     def kernel(
-        ocean_in, atm_in, flux_ref, weight_in, surf_in, slot_row, slot_col, omat, amat, coef, wet,
-        ocean_out, atm_out, flux_out,
-        ocean, atm, wbuf, prod, part, precv, surf, gathered, forced, ou, au, sst,
+        atm_in, ocean_in, flux_in, offset_in, tile_in, weight_in, air_mix, sea_mix, response,
+        factor, profile, sea,
+        atm_out, ocean_out, flux_out,
+        ocean_load, atm_load, ocean, atm, wbuf, prod, part, precv, surf, gathered, flux_ref,
+        pick_ref, wanted, omat, amat, coef, wet, ou, au, sst,
         orow, ocol, oedge, arow, acol, aedge,
-        in_sem, w_sem, surf_send, surf_recv, part_send, part_recv,
+        in_sem, ol_sem, al_sem, w_sem, surf_send, surf_recv, part_send, part_recv,
         o_send, o_recv, a_send, a_recv,
     ):
         ci = lax.axis_index("comp")
@@ -69,10 +62,17 @@
                 "lev": jnp.clip(li + dj, 0, lev_count - 1),
             }
 
-        load_ocean = pltpu.make_async_copy(ocean_in, ocean, in_sem.at[0])
-        load_atm = pltpu.make_async_copy(atm_in, atm, in_sem.at[1])
-        load_ocean.start()
-        load_atm.start()
+        loads = [
+            pltpu.make_async_copy(
+                source.at[:, pl.ds(128 * h, 128)], target.at[h], sem.at[h]
+            )
+            for source, target, sem in (
+                (ocean_in, ocean_load, ol_sem), (atm_in, atm_load, al_sem)
+            )
+            for h in range(target.shape[0])
+        ]
+        for load in loads:
+            load.start()
 
         def load_weight(y):
             return pltpu.make_async_copy(weight_in.at[y], wbuf.at[y], w_sem.at[y])
@@ -83,12 +83,11 @@
 
         lax.fori_loop(0, rows, start_weight, 0)
 
-        surf[4] = surf_in[...]
         for n, (di, dj) in enumerate(NEAR):
             if n != 4:
                 @pl.when(jnp.logical_not(there(di, dj)))
                 def _():
-                    surf[n] = jnp.zeros_like(surf_in)
+                    surf[n] = jnp.zeros(surf.shape[1:], BF16)
         for side, (di, dj) in enumerate(SIDES):
             @pl.when(jnp.logical_not(there(di, dj)))
             def _():
@@ -172,10 +171,107 @@
             width = state.shape[2]
             return lambda r: (state[r, :, 0:128], state[r, :, width - 128:width])
 
-        load_ocean.wait()
+        def turned(source, state, levels):
+            depth, width = state.shape[1:]
+            for r in range(rows):
+                for col in range(0, width, 128):
+                    state[r, 0:levels, col:col + 128] = source[
+                        col // 128, pl.ds(r, levels, stride=rows), :
+                    ]
+                if depth > levels:
+                    state[r, levels:depth] = jnp.zeros((depth - levels, width), F32)
+
+        for load in loads[:ocean_load.shape[0]]:
+            load.wait()
+        turned(ocean_load, ocean, sea_levels)
+        for h in range(ocean_load.shape[0]):
+            surf[4, :, 128 * h:128 * (h + 1)] = ocean_load[h, 0:rows].astype(BF16)
         pack(ends(ocean), oedge)
-        load_atm.wait()
+        for load in loads[ocean_load.shape[0]:]:
+            load.wait()
+        turned(atm_load, atm, last + 1)
         pack(ends(atm), aedge)
+
+        def one_hot(shape, test):
+            first = lax.broadcasted_iota(jnp.int32, shape, 0)
+            second = lax.broadcasted_iota(jnp.int32, shape, 1)
+            return test(first, second).astype(F32).astype(BF16)
+
+        def placed(matrix, width, places):
+            total = None
+            for term, offsets in zip(halves(matrix), places):
+                def test(k, j):
+                    hit = j == k + offsets[0]
+                    for offset in offsets[1:]:
+                        hit = jnp.logical_or(hit, j == k + offset)
+                    return hit
+
+                piece = jnp.dot(
+                    term, one_hot((matrix.shape[1], width), test), preferred_element_type=F32
+                )
+                total = piece if total is None else total + piece
+            return total
+
+        deep, high = ocean.shape[1], atm.shape[1]
+        wide_o, wide_a = omat.shape[1], amat.shape[1]
+        square = jnp.concatenate(
+            [
+                placed(sea_mix[...], wide_o, ((0, 2 * deep), (deep,)))
+                + placed(
+                    profile[...], wide_o,
+                    ((3 * deep, 3 * deep + 2 * chan), (3 * deep + chan,)),
+                ),
+                jnp.zeros((deep - sea_levels, wide_o), F32),
+            ],
+            axis=0,
+        )
+        omat[...] = square.astype(BF16)
+        both = jnp.concatenate(
+            [
+                air_mix[...],
+                jnp.dot(
+                    response[...], air_mix[...], precision=lax.Precision.HIGHEST,
+                    preferred_element_type=F32,
+                ),
+            ],
+            axis=0,
+        )
+        amat[...] = placed(both, wide_a, ((0, 2 * high), (high,))).astype(BF16)
+        field = lax.broadcasted_iota(jnp.int32, (chan, cells_a), 0)
+        factors = LINK * jnp.broadcast_to(response[:, last:last + 1], (chan, cells_a))
+        for c in range(chan):
+            factors = factors + jnp.where(field == c, factor[c], 0.0)
+        coef[...] = factors
+        wet[...] = sea[...].astype(F32)
+
+        spot = one_hot(
+            (rows * chan * per_tile, chan * rows),
+            lambda k, j: j == (k // per_tile) % chan * rows + k // (per_tile * chan),
+        )
+        flux_ref[...] = jnp.dot(
+            spot, flux_in[...], preferred_element_type=F32
+        ).astype(BF16).reshape(rows, chan * per_tile, cells_a)
+
+        slots = 9 * rows
+        offset = offset_in[...]
+        step_row = (offset >= 3).astype(jnp.int32) + (offset >= 6).astype(jnp.int32)
+        dest_row = reflect(ci + step_row - 1, comp_count)
+        dest_col = reflect(li + (offset - 3 * step_row) - 1, lev_count)
+        slot = ((dest_row - ci + 1) * 3 + (dest_col - li + 1)) * rows + tile_in[...]
+        pick_ref[...] = (
+            lax.broadcasted_iota(jnp.int32, (slots, pairs), 0) == slot
+        ).astype(F32).astype(BF16)
+        group = 16
+        owner = one_hot(
+            (rows * group, pairs),
+            lambda k, q: jnp.logical_and(
+                q == k // group * per_tile + k % group, k % group < per_tile
+            ),
+        )
+        wanted[...] = lax.dot_general(
+            owner, pick_ref[...], (((1,), (1,)), ((), ())), preferred_element_type=F32
+        ).astype(BF16)
+
         pl.semaphore_wait(barrier, tall * wide - 1)
 
         for n, (di, dj) in enumerate(NEAR):
@@ -202,11 +298,7 @@
 
         lax.fori_loop(0, rows, multiply, 0)
 
-        slots = 9 * rows
-        pick = (
-            lax.broadcasted_iota(jnp.int32, (slots, pairs), 0) == slot_row[...]
-        ).astype(F32).astype(BF16)
-        pick = jnp.concatenate([pick, pick], axis=1)
+        pick = jnp.concatenate([pick_ref[...], pick_ref[...]], axis=1)
         for c in range(chan):
             hi, lo = halves(prod[c])
             sums = jnp.dot(
@@ -225,11 +317,7 @@
                 @pl.when(there(-di, -dj))
                 def _():
                     surf_copy(n).wait_recv()
-        group = 16
-        wanted = (
-            lax.broadcasted_iota(jnp.int32, (rows * group, slots), 1) == slot_col[...]
-        ).astype(F32).astype(BF16)
-        found = jnp.dot(wanted, surf[...].reshape(slots, cells_o), preferred_element_type=F32)
+        found = jnp.dot(wanted[...], surf[...].reshape(slots, cells_o), preferred_element_type=F32)
         spare = lax.broadcasted_iota(jnp.int32, (rows * group, cells_o), 0) % group >= per_tile
         gathered[...] = jnp.where(spare, 1.0, found).astype(BF16).reshape(rows, group, cells_o)
         line = lax.broadcasted_iota(jnp.int32, (8, cells_a), 0)
@@ -326,7 +414,6 @@
                     ou[r, mixing:mixing + size] = both[r]
 
             wait_sides(ocean_parts, s)
-            deep = ocean.shape[1]
             for r in range(rows):
                 hi, lo = halves(stencil(ocean_parts, s, r))
                 ou[r, 0:3 * deep] = jnp.concatenate([hi, hi, lo], axis=0)
@@ -377,8 +464,6 @@
 ):
     comp_count = lax.axis_size("comp")
     lev_count = lax.axis_size("lev")
-    row_block = lax.axis_index("comp")
-    col_block = lax.axis_index("lev")
     pairs, cells_a, cells_o = pair_weight.shape
     air, rows = atm_state.shape[:2]
     sea = ocean_state.shape[0]
@@ -386,47 +471,23 @@
     per_tile = pairs // rows
     deep = (sea + 15) // 16 * 16
     high = (air + chan + 15) // 16 * 16
-
-    dest_row = reflect(row_block + pair_offset // 3 - 1, comp_count)
-    dest_col = reflect(col_block + pair_offset % 3 - 1, lev_count)
-    slot = ((dest_row - row_block + 1) * 3 + (dest_col - col_block + 1)) * rows + pair_tile
-    slot_col = jnp.pad(
-        slot.reshape(rows, per_tile), ((0, 0), (0, 16 - per_tile)), constant_values=-1
-    ).reshape(rows * 16, 1)
-
-    ocean_t = jnp.pad(ocean_state.transpose(1, 0, 2), ((0, 0), (0, deep - sea), (0, 0)))
-    atm_t = jnp.pad(atm_state.transpose(1, 0, 2), ((0, 0), (0, high - air), (0, 0)))
-    flux_t = jnp.repeat(flux_prev.transpose(1, 0, 2), per_tile, axis=1)
-    surface = ocean_state[0].astype(BF16)
-
-    omix_hi, omix_lo = split_outside(padded(ocean_mix, deep, deep))
-    depth_hi, depth_lo = split_outside(padded(depth_profile, deep, chan))
-    omat = jnp.concatenate(
-        [omix_hi, omix_lo, omix_hi, depth_hi, depth_lo, depth_hi, jnp.zeros_like(depth_hi)], axis=1
-    )
-    response = jnp.dot(exchange_response_matrix, atm_mix, precision=lax.Precision.HIGHEST)
-    amix_hi, amix_lo = split_outside(
-        padded(jnp.concatenate([atm_mix, response], axis=0), high, high)
-    )
-    amat = jnp.concatenate([amix_hi, amix_lo, amix_hi], axis=1)
-    coef = jnp.broadcast_to(
-        (exchange_factor_array + LINK * exchange_response_matrix[:, air - 1])[:, None],
-        (chan, cells_a),
-    )
-    dims = (rows, per_tile, chan, cells_a, cells_o, air - 1, (comp_count, lev_count))
+    dims = (rows, per_tile, chan, cells_a, cells_o, air - 1, sea, (comp_count, lev_count))
     anywhere = pl.BlockSpec(memory_space=pl.ANY)
     vmem = pl.BlockSpec(memory_space=pltpu.VMEM)
     dma = pltpu.SemaphoreType.DMA
-    ocean_end, atm_end, flux_end = pl.pallas_call(
+    smem = pl.BlockSpec(memory_space=pltpu.SMEM)
+    atm_end, ocean_end, flux_end = pl.pallas_call(
         make_kernel(dims),
         out_shape=(
+            jax.ShapeDtypeStruct((rows, high, cells_a), F32),
             jax.ShapeDtypeStruct((rows, deep, cells_o), F32),
-            jax.ShapeDtypeStruct((rows, high, cells_a), F32),
             jax.ShapeDtypeStruct((rows, chan, cells_a), F32),
         ),
-        in_specs=[anywhere, anywhere, vmem, anywhere] + [vmem] * 7,
+        in_specs=[anywhere, anywhere, vmem, vmem, vmem, anywhere, vmem, vmem, vmem, smem, vmem, vmem],
         out_specs=(anywhere, anywhere, vmem),
         scratch_shapes=[
+            pltpu.VMEM((cells_o // 128, sea * rows, 128), F32),
+            pltpu.VMEM((cells_a // 128, air * rows, 128), F32),
             pltpu.VMEM((rows, deep, cells_o), F32),
             pltpu.VMEM((rows, high, cells_a), F32),
             pltpu.VMEM((rows, per_tile * cells_a, cells_o), BF16),
@@ -435,7 +496,13 @@
             pltpu.VMEM((9, chan, rows, cells_o), BF16),
             pltpu.VMEM((9, rows, cells_o), BF16),
             pltpu.VMEM((rows, 16, cells_o), BF16),
-            pltpu.VMEM((8, 128), F32),
+            pltpu.VMEM((rows, chan * per_tile, cells_a), BF16),
+            pltpu.VMEM((9 * rows, pairs), BF16),
+            pltpu.VMEM((rows * 16, 9 * rows), BF16),
+            pltpu.VMEM((deep, 3 * deep + 4 * chan), BF16),
+            pltpu.VMEM((high, 3 * high), BF16),
+            pltpu.VMEM((chan, cells_a), F32),
+            pltpu.VMEM((rows, cells_o), F32),
             pltpu.VMEM((rows, 3 * deep + 4 * chan, cells_o), BF16),
             pltpu.VMEM((rows, 3 * high, cells_a), BF16),
             pltpu.VMEM((rows, 8, cells_a), F32),
@@ -446,6 +513,8 @@
             pltpu.VMEM((STEPS, 2, high, 128), F32),
             pltpu.VMEM((2, high, 128), F32),
             dma((2,)),
+            dma((cells_o // 128,)),
+            dma((cells_a // 128,)),
             dma((rows,)),
             dma((9,)),
             dma((9,)),
@@ -461,9 +530,13 @@
         ),
         name="coupled",
     )(
-        ocean_t, atm_t, flux_t,
+        atm_state.reshape(air * rows, cells_a),
+        ocean_state.reshape(sea * rows, cells_o),
+        flux_prev.reshape(chan * rows, cells_a),
+        pair_offset.reshape(1, pairs),
+        pair_tile.reshape(1, pairs),
         pair_weight.reshape(rows, per_tile * cells_a, cells_o),
-        surface, slot.reshape(1, pairs), slot_col, omat, amat, coef, sea_mask.astype(F32),
+        atm_mix, ocean_mix, exchange_response_matrix, exchange_factor_array, depth_profile, sea_mask,
     )
     return (
         atm_end[:, :air].transpose(1, 0, 2),

time: 53.1 us -> 50.6 us (0.953)
  other arithmetic: 4.61 us -> 0.01 us
  local copies, waits for them, and re-layouts: 12.4 us -> 15.2 us
  matrix products: 0.92 us -> 0 us
    unnamed x8 -> x26, local copies, waits for them, and re-layouts: 10.3 us -> 15.1 us
    convert_element_type x4 -> x0, other arithmetic: 2.29 us -> none  [the longest x3 1.57 us: split_outside(): return (hi.astype(BF16), (x - hi).astype(BF16))]
    add x2 -> x0, other arithmetic: 1.36 us -> none  [the longest x1 0.7 us: body(): ((dest_row - row_block + 1) * 3 + (dest_col - col_block + 1)) * rows]
    dot_general x1 -> x0, matrix products: 0.92 us -> none  [body(): jnp.dot(exchange_response_matrix, atm_mix, precision=lax.Precision.HIGHEST)]
    mul x1 -> x0, other arithmetic: 0.87 us -> none  [body(): LINK * exchange_response_matrix[:, air - 1]]
    transpose x1 -> x0, local copies, waits for them, and re-layouts: 0.77 us -> none  [body(): flux_t = jnp.repeat(flux_prev.transpose(1, 0, 2), per_tile, axis=1)]
    convert_element_type x1 -> x0, local copies, waits for them, and re-layouts: 0.73 us -> none  [body(): surface = ocean_state[0].astype(BF16)]
where the time goes in v2:
time: 50.6 us; the launch traced here: 50 us
  Pallas kernels  34.1 us (67%)
  local copies, waits for them, and re-layouts  15.2 us (30%)
  between operations  0.67 us (1%)
    pallas_call x1, Pallas kernels, body(): pl.pallas_call(make_kernel(dims), out_shape=(jax.ShapeDtypeStruct((rows,...  34.1 us
    unnamed x26, local copies, waits for them, and re-layouts  15.1 us

profile of v2, /device:TPU:0, one launch (start us, length us, event | category | flops | bytes accessed | tf_op | source)
XLA Modules:
  0.0 50.0 jit_solution(3525966221778412348)
XLA Ops:
  0.6 0.8 %copy.15.profile = f32[60,8]{1,0:T(8,128)S(1)} copy(f32[60,8]{0,1:T(8,128)} %param.22) | data formatting | bytes 3840 | tf_op args[10]
  1.4 0.0 copy-start
  1.4 3.4 %copy-done = bf16[128,128,256]{2,1,0:T(8,128)(2,1)S(1)} copy-done((bf16[128,128,256]{2,1,0:T(8,128)(2,1)S(1)}, bf16[128,128,256]{2,1,0:T(8,128)(2,1)}, u32[]{:S(2)}) %copy-start) | copy-done | bytes 8388632
  4.8 0.0 copy-start.1
  4.8 1.2 %copy-done.1 = f32[60,16,256]{2,1,0:T(8,128)S(1)} copy-done((f32[60,16,256]{2,1,0:T(8,128)S(1)}, f32[60,16,256]{2,1,0:T(8,128)}, u32[]{:S(2)}) %copy-start.1) | copy-done | bytes 983064
  6.0 0.0 copy-start.2
  6.0 1.1 %copy-done.2 = f32[72,16,128]{2,1,0:T(8,128)S(1)} copy-done((f32[72,16,128]{2,1,0:T(8,128)S(1)}, f32[72,16,128]{2,1,0:T(8,128)}, u32[]{:S(2)}) %copy-start.2) | copy-done | bytes 589848
  7.1 0.0 copy-start.3
  7.1 0.8 %copy-done.3 = f32[72,72]{1,0:T(8,128)S(1)} copy-done((f32[72,72]{1,0:T(8,128)S(1)}, f32[72,72]{1,0:T(8,128)}, u32[]{:S(2)}) %copy-start.3) | copy-done | bytes 20760
  7.8 0.0 copy-start.4
  7.8 0.8 %copy-done.4 = bf16[8,16,128]{2,1,0:T(8,128)(2,1)S(1)} copy-done((bf16[8,16,128]{2,1,0:T(8,128)(2,1)S(1)}, bf16[8,16,128]{2,1,0:T(8,128)(2,1)}, u32[]{:S(2)}) %copy-start.4) | copy-done | bytes 32792
  8.6 0.0 copy-start.5
  8.6 0.8 %copy-done.5 = f32[60,60]{1,0:T(8,128)S(1)} copy-done((f32[60,60]{1,0:T(8,128)S(1)}, f32[60,60]{1,0:T(8,128)}, u32[]{:S(2)}) %copy-start.5) | copy-done | bytes 14424
  9.3 0.0 copy-start.6
  9.3 0.7 %copy-done.6 = s32[16,256]{1,0:T(8,128)S(1)} copy-done((s32[16,256]{1,0:T(8,128)S(1)}, s32[16,256]{1,0:T(8,128)}, u32[]{:S(2)}) %copy-start.6) | copy-done | bytes 16408
  10.1 0.0 copy-start.7
  10.1 0.7 %copy-done.7 = f32[8,72]{1,0:T(8,128)S(1)} copy-done((f32[8,72]{1,0:T(8,128)S(1)}, f32[8,72]{1,0:T(8,128)}, u32[]{:S(2)}) %copy-start.7) | copy-done | bytes 2328
  10.8 0.0 copy-start.8
  10.8 0.7 %copy-done.8 = s32[128]{0:T(128)S(1)} copy-done((s32[128]{0:T(128)S(1)}, s32[128]{0:T(128)}, u32[]{:S(2)}) %copy-start.8) | copy-done | bytes 536
  11.4 0.0 copy-start.9
  11.4 0.7 %copy-done.9 = s32[128]{0:T(128)S(1)} copy-done((s32[128]{0:T(128)S(1)}, s32[128]{0:T(128)}, u32[]{:S(2)}) %copy-start.9) | copy-done | bytes 536
  12.1 0.0 copy-start.10
  12.1 0.7 %copy-done.10 = f32[8]{0:T(128)S(1)} copy-done((f32[8]{0:T(128)S(1)}, f32[8]{0:T(128)}, u32[]{:S(2)}) %copy-start.10) | copy-done | bytes 56
  12.7 34.1 %coupled.1 = (f32[16,80,128]{2,1,0:T(8,128)S(1)}, f32[16,64,256]{2,1,0:T(8,128)S(1)}, f32[16,8,128]{2,1,0:T(8,128)S(1)}) custom-call(f32[1152,128]{1,0:T(8,128)S(1)} %bitcast.14, f32[960,256]{1,0:T(8,128)S(1)} %bitcast.13, bf16[128,128]{1,0:T(8,128)(2,1)S(1)} %bitcast.15, s32[1,128]{1,0:T(1,128)S(1)} %bitcast.16, s32[1,128]{1,0:T(1,128)S(1)} %bitcast.17, ...), custom_call_target="tpu_custom_call" | custom-call | tf_op jit(solution)/shard_map/coupled/pallas_call | solution.py:479
  46.9 0.9 %copy.16 = f32[72,16,128]{2,1,0:T(8,128)} copy(f32[72,16,128]{2,0,1:T(8,128)S(1)} %slice_bitcast_fusion.1) | data formatting | bytes 1179648
  47.8 0.6 %copy.18 = bf16[8,16,128]{2,1,0:T(8,128)(2,1)} copy(bf16[8,16,128]{2,0,1:T(8,128)(2,1)S(1)} %fusion) | data formatting | bytes 65536
  48.5 0.1 slice_bitcast_fusion
  48.5 1.5 %copy.17 = f32[60,16,256]{2,1,0:T(8,128)} copy(f32[60,16,256]{2,0,1:T(8,128)S(1)} %slice_bitcast_fusion) | data formatting | bytes 1966080
  (2 shorter events, 0.0 us)
Async XLA Ops:
  1.4 3.4 %copy-start = (bf16[128,128,256]{2,1,0:T(8,128)(2,1)S(1)}, bf16[128,128,256]{2,1,0:T(8,128)(2,1)}, u32[]{:S(2)}) copy-start(bf16[128,128,256]{2,1,0:T(8,128)(2,1)} %param.17) | copy-start | bytes 25165828
  4.8 1.2 %copy-start.1 = (f32[60,16,256]{2,1,0:T(8,128)S(1)}, f32[60,16,256]{2,1,0:T(8,128)}, u32[]{:S(2)}) copy-start(f32[60,16,256]{2,1,0:T(8,128)} %param.13) | copy-start | bytes 2949124
  6.0 1.1 %copy-start.2 = (f32[72,16,128]{2,1,0:T(8,128)S(1)}, f32[72,16,128]{2,1,0:T(8,128)}, u32[]{:S(2)}) copy-start(f32[72,16,128]{2,1,0:T(8,128)} %param.12) | copy-start | bytes 1769476
  7.1 0.8 %copy-start.3 = (f32[72,72]{1,0:T(8,128)S(1)}, f32[72,72]{1,0:T(8,128)}, u32[]{:S(2)}) copy-start(f32[72,72]{1,0:T(8,128)} %air_mix.1) | copy-start | bytes 62212
  7.8 0.8 %copy-start.4 = (bf16[8,16,128]{2,1,0:T(8,128)(2,1)S(1)}, bf16[8,16,128]{2,1,0:T(8,128)(2,1)}, u32[]{:S(2)}) copy-start(bf16[8,16,128]{2,1,0:T(8,128)(2,1)} %param.14) | copy-start | bytes 98308
  8.6 0.8 %copy-start.5 = (f32[60,60]{1,0:T(8,128)S(1)}, f32[60,60]{1,0:T(8,128)}, u32[]{:S(2)}) copy-start(f32[60,60]{1,0:T(8,128)} %sea_mix.1) | copy-start | bytes 43204
  9.3 0.7 %copy-start.6 = (s32[16,256]{1,0:T(8,128)S(1)}, s32[16,256]{1,0:T(8,128)}, u32[]{:S(2)}) copy-start(s32[16,256]{1,0:T(8,128)} %sea.1) | copy-start | bytes 49156
  10.1 0.7 %copy-start.7 = (f32[8,72]{1,0:T(8,128)S(1)}, f32[8,72]{1,0:T(8,128)}, u32[]{:S(2)}) copy-start(f32[8,72]{1,0:T(8,128)} %response.1) | copy-start | bytes 6916
  10.8 0.7 %copy-start.8 = (s32[128]{0:T(128)S(1)}, s32[128]{0:T(128)}, u32[]{:S(2)}) copy-start(s32[128]{0:T(128)} %param.15) | copy-start | bytes 1540
  11.4 0.7 %copy-start.9 = (s32[128]{0:T(128)S(1)}, s32[128]{0:T(128)}, u32[]{:S(2)}) copy-start(s32[128]{0:T(128)} %param.16) | copy-start | bytes 1540
  12.1 0.7 %copy-start.10 = (f32[8]{0:T(128)S(1)}, f32[8]{0:T(128)}, u32[]{:S(2)}) copy-start(f32[8]{0:T(128)} %factor.1) | copy-start | bytes 100

commit v3 on v2

--- a/solution.py
+++ b/solution.py
@@ -31,13 +31,14 @@
     pairs = rows * per_tile
 
     def kernel(
-        atm_in, ocean_in, flux_in, offset_in, tile_in, weight_in, air_mix, sea_mix, response,
-        factor, profile, sea,
+        atm_in, ocean_in, flux_far, offset_far, tile_far, weight_in, air_far, sea_far,
+        response_far, factor_far, profile_far, mask_far,
         atm_out, ocean_out, flux_out,
+        flux_in, offset_in, tile_in, air_mix, sea_mix, response, factor, profile, sea,
         ocean_load, atm_load, ocean, atm, wbuf, prod, part, precv, surf, gathered, flux_ref,
         pick_ref, wanted, omat, amat, coef, wet, ou, au, sst,
         orow, ocol, oedge, arow, acol, aedge,
-        in_sem, ol_sem, al_sem, w_sem, surf_send, surf_recv, part_send, part_recv,
+        in_sem, small_sem, ol_sem, al_sem, w_sem, surf_send, surf_recv, part_send, part_recv,
         o_send, o_recv, a_send, a_recv,
     ):
         ci = lax.axis_index("comp")
@@ -73,6 +74,16 @@
         ]
         for load in loads:
             load.start()
+        small = [
+            pltpu.make_async_copy(source, target, small_sem.at[k])
+            for k, (source, target) in enumerate((
+                (flux_far, flux_in), (offset_far, offset_in), (tile_far, tile_in),
+                (air_far, air_mix), (sea_far, sea_mix), (response_far, response),
+                (factor_far, factor), (profile_far, profile), (mask_far, sea),
+            ))
+        ]
+        for load in small:
+            load.start()
 
         def load_weight(y):
             return pltpu.make_async_copy(weight_in.at[y], wbuf.at[y], w_sem.at[y])
@@ -137,8 +148,10 @@
         ocean_parts = (ocean, orow, ocol, oedge, o_send, o_recv)
         atm_parts = (atm, arow, acol, aedge, a_send, a_recv)
 
-        def start_sides(parts, s):
-            for side, (di, dj) in enumerate(SIDES):
+        def start_sides(parts, s, sides=(0, 1, 2, 3)):
+            for side in sides:
+                di, dj = SIDES[side]
+
                 @pl.when(there(di, dj))
                 def _():
                     side_copy(*parts, s, side).start()
@@ -149,8 +162,10 @@
                 def _():
                     side_copy(*parts, s, side).wait_send()
 
-        def wait_sides(parts, s):
-            for side, (di, dj) in enumerate(SIDES):
+        def wait_sides(parts, s, sides):
+            for side in sides:
+                di, dj = SIDES[side]
+
                 @pl.when(there(-di, -dj))
                 def _():
                     side_copy(*parts, s, side).wait_recv()
@@ -192,12 +207,15 @@
         turned(atm_load, atm, last + 1)
         pack(ends(atm), aedge)
 
+        for load in small:
+            load.wait()
+
         def one_hot(shape, test):
             first = lax.broadcasted_iota(jnp.int32, shape, 0)
             second = lax.broadcasted_iota(jnp.int32, shape, 1)
             return test(first, second).astype(F32).astype(BF16)
 
-        def placed(matrix, width, places):
+        def placed(matrix, width, places, inner=1):
             total = None
             for term, offsets in zip(halves(matrix), places):
                 def test(k, j):
@@ -206,8 +224,9 @@
                         hit = jnp.logical_or(hit, j == k + offset)
                     return hit
 
-                piece = jnp.dot(
-                    term, one_hot((matrix.shape[1], width), test), preferred_element_type=F32
+                piece = lax.dot_general(
+                    term, one_hot((matrix.shape[inner], width), test),
+                    (((inner,), (0,)), ((), ())), preferred_element_type=F32,
                 )
                 total = piece if total is None else total + piece
             return total
@@ -219,7 +238,7 @@
                 placed(sea_mix[...], wide_o, ((0, 2 * deep), (deep,)))
                 + placed(
                     profile[...], wide_o,
-                    ((3 * deep, 3 * deep + 2 * chan), (3 * deep + chan,)),
+                    ((3 * deep, 3 * deep + 2 * chan), (3 * deep + chan,)), 0,
                 ),
                 jnp.zeros((deep - sea_levels, wide_o), F32),
             ],
@@ -360,23 +379,39 @@
             return (1.0 - 4.0 * RATE) * x + RATE * ((up + down) + (west_end + east_end))
 
         def step(s, carry):
-            wait_sides(atm_parts, s)
-            for r in range(rows):
+            def spread_atm(r):
                 hi, lo = halves(stencil(atm_parts, s, r))
                 au[r] = jnp.concatenate([hi, hi, lo], axis=0)
+
+            wait_sides(atm_parts, s, (2, 3))
+            for r in range(1, rows - 1):
+                spread_atm(r)
+            wait_sides(atm_parts, s, (0, 1))
+            spread_atm(0)
+            spread_atm(rows - 1)
             wait_sent(atm_parts, s)
             depth = atm.shape[1]
             level = lax.broadcasted_iota(jnp.int32, (depth, cells_a), 0)
-            for r in range(rows):
+            def mix_atm(r):
                 mixed = jnp.dot(amat[...], au[r], preferred_element_type=F32)
                 gap = sst[r, 0:1] - mixed[last:last + 1]
                 flux_out[r] += mixed[last + 1:last + 1 + chan] + coef[...] * gap
                 atm[r] = mixed + jnp.where(level == last, LINK * gap, 0.0)
 
+            mix_atm(0)
+            mix_atm(rows - 1)
+
+            @pl.when(s < STEPS - 1)
+            def _():
+                start_sides(atm_parts, s + 1, (0, 1))
+
+            for r in range(1, rows - 1):
+                mix_atm(r)
+
             @pl.when(s < STEPS - 1)
             def _():
                 pack(ends(atm), aedge)
-                start_sides(atm_parts, s + 1)
+                start_sides(atm_parts, s + 1, (2, 3))
 
             @pl.when(s == 0)
             def _():
@@ -413,20 +448,36 @@
                 for r in range(rows):
                     ou[r, mixing:mixing + size] = both[r]
 
-            wait_sides(ocean_parts, s)
-            for r in range(rows):
+            def spread_ocean(r):
                 hi, lo = halves(stencil(ocean_parts, s, r))
                 ou[r, 0:3 * deep] = jnp.concatenate([hi, hi, lo], axis=0)
-            wait_sent(ocean_parts, s)
-            for r in range(rows):
+
+            def mix_ocean(r):
                 ocean[r] = wet[r:r + 1] * jnp.dot(
                     omat[...], ou[r], preferred_element_type=F32
                 )
 
+            wait_sides(ocean_parts, s, (2, 3))
+            for r in range(1, rows - 1):
+                spread_ocean(r)
+            wait_sides(ocean_parts, s, (0, 1))
+            spread_ocean(0)
+            spread_ocean(rows - 1)
+            wait_sent(ocean_parts, s)
+            mix_ocean(0)
+            mix_ocean(rows - 1)
+
+            @pl.when(s < STEPS - 1)
+            def _():
+                start_sides(ocean_parts, s + 1, (0, 1))
+
+            for r in range(1, rows - 1):
+                mix_ocean(r)
+
             @pl.when(s < STEPS - 1)
             def _():
                 pack(ends(ocean), oedge)
-                start_sides(ocean_parts, s + 1)
+                start_sides(ocean_parts, s + 1, (2, 3))
 
             return carry
 
@@ -475,7 +526,6 @@
     anywhere = pl.BlockSpec(memory_space=pl.ANY)
     vmem = pl.BlockSpec(memory_space=pltpu.VMEM)
     dma = pltpu.SemaphoreType.DMA
-    smem = pl.BlockSpec(memory_space=pltpu.SMEM)
     atm_end, ocean_end, flux_end = pl.pallas_call(
         make_kernel(dims),
         out_shape=(
@@ -483,9 +533,18 @@
             jax.ShapeDtypeStruct((rows, deep, cells_o), F32),
             jax.ShapeDtypeStruct((rows, chan, cells_a), F32),
         ),
-        in_specs=[anywhere, anywhere, vmem, vmem, vmem, anywhere, vmem, vmem, vmem, smem, vmem, vmem],
+        in_specs=[anywhere] * 12,
         out_specs=(anywhere, anywhere, vmem),
         scratch_shapes=[
+            pltpu.VMEM((chan * rows, cells_a), BF16),
+            pltpu.VMEM((1, pairs), jnp.int32),
+            pltpu.VMEM((1, pairs), jnp.int32),
+            pltpu.VMEM((air, air), F32),
+            pltpu.VMEM((sea, sea), F32),
+            pltpu.VMEM((chan, air), F32),
+            pltpu.SMEM((chan,), F32),
+            pltpu.VMEM((chan, sea), F32),
+            pltpu.VMEM((rows, cells_o), jnp.int32),
             pltpu.VMEM((cells_o // 128, sea * rows, 128), F32),
             pltpu.VMEM((cells_a // 128, air * rows, 128), F32),
             pltpu.VMEM((rows, deep, cells_o), F32),
@@ -513,6 +572,7 @@
             pltpu.VMEM((STEPS, 2, high, 128), F32),
             pltpu.VMEM((2, high, 128), F32),
             dma((2,)),
+            dma((9,)),
             dma((cells_o // 128,)),
             dma((cells_a // 128,)),
             dma((rows,)),
@@ -526,7 +586,7 @@
             dma((STEPS, 4)),
         ],
         compiler_params=pltpu.CompilerParams(
-            collective_id=0, has_side_effects=True, vmem_limit_bytes=40 * 1024 * 1024
+            collective_id=0, has_side_effects=True, vmem_limit_bytes=60 * 1024 * 1024
         ),
         name="coupled",
     )(
@@ -536,7 +596,8 @@
         pair_offset.reshape(1, pairs),
         pair_tile.reshape(1, pairs),
         pair_weight.reshape(rows, per_tile * cells_a, cells_o),
-        atm_mix, ocean_mix, exchange_response_matrix, exchange_factor_array, depth_profile, sea_mask,
+        atm_mix, ocean_mix, exchange_response_matrix, exchange_factor_array,
+        depth_profile.T, sea_mask,
     )
     return (
         atm_end[:, :air].transpose(1, 0, 2),

time: 50.6 us -> 40.1 us (0.79)
  the two profiles are of different devices: /device:TPU:0 before, /device:TPU:1 now
where the time goes in v3:
time: 40.1 us; the launch traced here: 39.8 us
  Pallas kernels  32.8 us (82%)
  local copies, waits for them, and re-layouts  5.49 us (14%)
  other arithmetic  0.84 us (2%)
  between operations  0.66 us (2%)
    pallas_call x1, Pallas kernels, body(): pl.pallas_call(make_kernel(dims), out_shape=(jax.ShapeDtypeStruct((rows,...  32.8 us
    unnamed x3, local copies, waits for them, and re-layouts  3.06 us
    transpose x1, local copies, waits for them, and re-layouts, body(): ocean_end[:, :sea].transpose(1, 0, 2)  1.31 us
    transpose x1, local copies, waits for them, and re-layouts, body(): atm_end[:, :air].transpose(1, 0, 2)  1.11 us
    convert_element_type x1, other arithmetic, body(): (flux_end / STEPS).transpose(1, 0, 2).astype(BF16)  0.84 us

profile of v3, /device:TPU:1, one launch (start us, length us, event | category | flops | bytes accessed | tf_op | source)
XLA Modules:
  0.0 39.8 jit_solution(8688452586715074591)
XLA Ops:
  0.6 32.8 %coupled.1 = (f32[16,80,128]{2,1,0:T(8,128)}, f32[16,64,256]{2,1,0:T(8,128)}, f32[16,8,128]{2,1,0:T(8,128)}) custom-call(f32[1152,128]{1,0:T(8,128)} %bitcast.15, f32[960,256]{1,0:T(8,128)} %bitcast.14, bf16[128,128]{1,0:T(8,128)(2,1)} %bitcast.16, s32[1,128]{1,0:T(1,128)} %bitcast.18, s32[1,128]{1,0:T(1,128)} %bitcast.19, bf16[16,1024,256]{2,1,0:T(8,128)(2,1)} %bitcast.13, ...), custom_call_target="tpu_custom_call" | custom-call | tf_op jit(solution)/shard_map/coupled/pallas_call | solution.py:529
  33.5 1.1 %slice_bitcast_fusion.1 = f32[72,16,128]{2,0,1:T(8,128)S(1)} fusion(f32[16,80,128]{2,1,0:T(8,128)} %get-tuple-element.6), kind=kLoop, calls=%fused_computation.1 | loop fusion | bytes 1179648 | tf_op jit(solution)/shard_map/transpose | solution.py:603
  34.6 0.9 %copy.15 = f32[72,16,128]{2,1,0:T(8,128)} copy(f32[72,16,128]{2,0,1:T(8,128)S(1)} %slice_bitcast_fusion.1) | data formatting | bytes 1179648
  35.5 0.8 %fusion = bf16[8,16,128]{2,0,1:T(8,128)(2,1)S(1)} fusion(f32[16,8,128]{2,1,0:T(8,128)} %get-tuple-element.8), kind=kLoop, calls=%fused_computation.3 | loop fusion | flops 32768 | bytes 98304 | tf_op jit(solution)/shard_map/convert_element_type | solution.py:605
  36.4 0.6 %copy.17 = bf16[8,16,128]{2,1,0:T(8,128)(2,1)} copy(bf16[8,16,128]{2,0,1:T(8,128)(2,1)S(1)} %fusion) | data formatting | bytes 65536
  37.0 1.3 %slice_bitcast_fusion = f32[60,16,256]{2,0,1:T(8,128)S(1)} fusion(f32[16,64,256]{2,1,0:T(8,128)} %get-tuple-element.7), kind=kLoop, calls=%fused_computation | loop fusion | bytes 1966080 | tf_op jit(solution)/shard_map/transpose | solution.py:604
  38.3 1.5 %copy.16 = f32[60,16,256]{2,1,0:T(8,128)} copy(f32[60,16,256]{2,0,1:T(8,128)S(1)} %slice_bitcast_fusion) | data formatting | bytes 1966080

commit v4 on v3

--- a/solution.py
+++ b/solution.py
@@ -33,8 +33,8 @@
     def kernel(
         atm_in, ocean_in, flux_far, offset_far, tile_far, weight_in, air_far, sea_far,
         response_far, factor_far, profile_far, mask_far,
-        atm_out, ocean_out, flux_out,
-        flux_in, offset_in, tile_in, air_mix, sea_mix, response, factor, profile, sea,
+        atm_out, ocean_out, flux_far_out,
+        flux_out, flux_sum, flux_end, flux_in, offset_in, tile_in, air_mix, sea_mix, response, factor, profile, sea,
         ocean_load, atm_load, ocean, atm, wbuf, prod, part, precv, surf, gathered, flux_ref,
         pick_ref, wanted, omat, amat, coef, wet, ou, au, sst,
         orow, ocol, oedge, arow, acol, aedge,
@@ -378,6 +378,21 @@
                 east_end = jnp.concatenate([east[:, 0:width - 128], east_end], axis=1)
             return (1.0 - 4.0 * RATE) * x + RATE * ((up + down) + (west_end + east_end))
 
+        def turned_back(state, target, levels):
+            for r in range(rows):
+                for h in range(target.shape[0]):
+                    target[h, pl.ds(r, levels, stride=rows), :] = state[
+                        r, 0:levels, 128 * h:128 * (h + 1)
+                    ]
+
+        def saves(source, target, sem):
+            return [
+                pltpu.make_async_copy(
+                    source.at[h], target.at[:, pl.ds(128 * h, 128)], sem.at[h]
+                )
+                for h in range(source.shape[0])
+            ]
+
         def step(s, carry):
             def spread_atm(r):
                 hi, lo = halves(stencil(atm_parts, s, r))
@@ -412,6 +427,12 @@
             def _():
                 pack(ends(atm), aedge)
                 start_sides(atm_parts, s + 1, (2, 3))
+
+            @pl.when(s == STEPS - 1)
+            def _():
+                turned_back(atm, atm_load, last + 1)
+                for save in saves(atm_load, atm_out, al_sem):
+                    save.start()
 
             @pl.when(s == 0)
             def _():
@@ -483,18 +504,23 @@
 
         lax.fori_loop(0, STEPS, step, 0)
 
-        save_ocean = pltpu.make_async_copy(ocean, ocean_out, in_sem.at[0])
-        save_atm = pltpu.make_async_copy(atm, atm_out, in_sem.at[1])
-        save_ocean.start()
-        save_atm.start()
+        turned_back(ocean, ocean_load, sea_levels)
+        for save in saves(ocean_load, ocean_out, ol_sem):
+            save.start()
+        for r in range(rows):
+            flux_sum[pl.ds(r, chan, stride=rows), :] = flux_out[r] * (1.0 / STEPS)
+        flux_end[...] = flux_sum[...].astype(BF16)
+        save_flux = pltpu.make_async_copy(flux_end, flux_far_out, in_sem.at[0])
+        save_flux.start()
         for n, (di, dj) in enumerate(NEAR):
             if n != 4:
                 @pl.when(there(di, dj))
                 def _():
                     surf_copy(n).wait_send()
                     part_copy(n).wait_send()
-        save_ocean.wait()
-        save_atm.wait()
+        save_flux.wait()
+        for save in saves(ocean_load, ocean_out, ol_sem) + saves(atm_load, atm_out, al_sem):
+            save.wait()
 
     return kernel
 
@@ -524,18 +550,20 @@
     high = (air + chan + 15) // 16 * 16
     dims = (rows, per_tile, chan, cells_a, cells_o, air - 1, sea, (comp_count, lev_count))
     anywhere = pl.BlockSpec(memory_space=pl.ANY)
-    vmem = pl.BlockSpec(memory_space=pltpu.VMEM)
     dma = pltpu.SemaphoreType.DMA
     atm_end, ocean_end, flux_end = pl.pallas_call(
         make_kernel(dims),
         out_shape=(
-            jax.ShapeDtypeStruct((rows, high, cells_a), F32),
-            jax.ShapeDtypeStruct((rows, deep, cells_o), F32),
-            jax.ShapeDtypeStruct((rows, chan, cells_a), F32),
+            jax.ShapeDtypeStruct((air * rows, cells_a), F32),
+            jax.ShapeDtypeStruct((sea * rows, cells_o), F32),
+            jax.ShapeDtypeStruct((chan * rows, cells_a), BF16),
         ),
         in_specs=[anywhere] * 12,
-        out_specs=(anywhere, anywhere, vmem),
+        out_specs=(anywhere, anywhere, anywhere),
         scratch_shapes=[
+            pltpu.VMEM((rows, chan, cells_a), F32),
+            pltpu.VMEM((chan * rows, cells_a), F32),
+            pltpu.VMEM((chan * rows, cells_a), BF16),
             pltpu.VMEM((chan * rows, cells_a), BF16),
             pltpu.VMEM((1, pairs), jnp.int32),
             pltpu.VMEM((1, pairs), jnp.int32),
@@ -571,7 +599,7 @@
             pltpu.VMEM((STEPS, 2, high, cells_a), F32),
             pltpu.VMEM((STEPS, 2, high, 128), F32),
             pltpu.VMEM((2, high, 128), F32),
-            dma((2,)),
+            dma((1,)),
             dma((9,)),
             dma((cells_o // 128,)),
             dma((cells_a // 128,)),
@@ -600,9 +628,9 @@
         depth_profile.T, sea_mask,
     )
     return (
-        atm_end[:, :air].transpose(1, 0, 2),
-        ocean_end[:, :sea].transpose(1, 0, 2),
-        (flux_end / STEPS).transpose(1, 0, 2).astype(BF16),
+        atm_end.reshape(air, rows, cells_a),
+        ocean_end.reshape(sea, rows, cells_o),
+        flux_end.reshape(chan, rows, cells_a),
     )
 
 

time: 40.1 us -> 38.9 us (0.970)
  other arithmetic: 0.84 us -> 0 us
    unnamed x3, local copies, waits for them, and re-layouts: 3.06 us -> 5.5 us
    transpose x2 -> x0, local copies, waits for them, and re-layouts: 2.42 us -> none  [the longest x1 1.31 us: body(): ocean_end[:, :sea].transpose(1, 0, 2)]
    convert_element_type x1 -> x0, other arithmetic: 0.84 us -> none  [body(): (flux_end / STEPS).transpose(1, 0, 2).astype(BF16)]
where the time goes in v4:
time: 38.9 us; the launch traced here: 38.6 us
  Pallas kernels  32.5 us (84%)
  local copies, waits for them, and re-layouts  5.5 us (14%)
  between operations  0.64 us (2%)
    pallas_call x1, Pallas kernels, body(): pl.pallas_call(make_kernel(dims), out_shape=(jax.ShapeDtypeStruct((air *...  32.5 us
    unnamed x3, local copies, waits for them, and re-layouts  5.5 us

profile of v4, /device:TPU:1, one launch (start us, length us, event | category | flops | bytes accessed | tf_op | source)
XLA Modules:
  0.0 38.6 jit_solution(698628567006773117)
XLA Ops:
  0.6 32.5 %coupled.1 = (f32[1152,128]{1,0:T(8,128)}, f32[960,256]{1,0:T(8,128)}, bf16[128,128]{1,0:T(8,128)(2,1)}) custom-call(f32[1152,128]{1,0:T(8,128)} %bitcast.13, f32[960,256]{1,0:T(8,128)} %bitcast.11, bf16[128,128]{1,0:T(8,128)(2,1)} %bitcast.15, s32[1,128]{1,0:T(1,128)} %bitcast.18, s32[1,128]{1,0:T(1,128)} %bitcast.19, bf16[16,1024,256]{2,1,0:T(8,128)(2,1)} %bitcast.10, ...), custom_call_target="tpu_custom_call" | custom-call | tf_op jit(solution)/shard_map/coupled/pallas_call | solution.py:554
  33.1 1.9 %copy.18 = f32[72,16,128]{2,1,0:T(8,128)} copy(f32[72,16,128]{2,1,0:T(8,128)} %bitcast.14) | data formatting | bytes 1179648
  35.1 2.2 %copy.19 = f32[60,16,256]{2,1,0:T(8,128)} copy(f32[60,16,256]{2,1,0:T(8,128)} %bitcast.12) | data formatting | bytes 1966080
  37.3 1.4 %copy.20 = bf16[8,16,128]{2,1,0:T(8,128)(2,1)} copy(bf16[8,16,128]{2,1,0:T(8,128)(2,1)} %bitcast.16) | data formatting | bytes 65536

commit v5 on v4

--- a/solution.py
+++ b/solution.py
@@ -315,7 +315,7 @@
                 prod[c, at, :] = out[c * per_tile:(c + 1) * per_tile]
             return carry
 
-        lax.fori_loop(0, rows, multiply, 0)
+        lax.fori_loop(0, rows, multiply, 0, unroll=2)
 
         pick = jnp.concatenate([pick_ref[...], pick_ref[...]], axis=1)
         for c in range(chan):
@@ -355,7 +355,7 @@
             sst[y] = jnp.broadcast_to(total, (8, cells_a)) / den
             return carry
 
-        lax.fori_loop(0, rows, regrid, 0)
+        lax.fori_loop(0, rows, regrid, 0, unroll=4)
         flux_out[...] = jnp.zeros_like(flux_out)
 
         def stencil(parts, s, r):

time: 38.9 us -> 39.7 us (1.021)
  Pallas kernels: 32.5 us -> 33.3 us
    pallas_call x1, Pallas kernels: 32.5 us -> 33.3 us  [body(): pl.pallas_call(make_kernel(dims), out_shape=(jax.ShapeDtypeStruct((air *...]
where the time goes in v5:
time: 39.7 us; the launch traced here: 39.4 us
  Pallas kernels  33.3 us (84%)
  local copies, waits for them, and re-layouts  5.5 us (14%)
  between operations  0.64 us (2%)
    pallas_call x1, Pallas kernels, body(): pl.pallas_call(make_kernel(dims), out_shape=(jax.ShapeDtypeStruct((air *...  33.3 us
    unnamed x3, local copies, waits for them, and re-layouts  5.5 us

profile of v5, /device:TPU:1, one launch (start us, length us, event | category | flops | bytes accessed | tf_op | source)
XLA Modules:
  0.0 39.4 jit_solution(7723218962152824768)
XLA Ops:
  0.6 33.3 %coupled.1 = (f32[1152,128]{1,0:T(8,128)}, f32[960,256]{1,0:T(8,128)}, bf16[128,128]{1,0:T(8,128)(2,1)}) custom-call(f32[1152,128]{1,0:T(8,128)} %bitcast.13, f32[960,256]{1,0:T(8,128)} %bitcast.11, bf16[128,128]{1,0:T(8,128)(2,1)} %bitcast.15, s32[1,128]{1,0:T(1,128)} %bitcast.18, s32[1,128]{1,0:T(1,128)} %bitcast.19, bf16[16,1024,256]{2,1,0:T(8,128)(2,1)} %bitcast.10, ...), custom_call_target="tpu_custom_call" | custom-call | tf_op jit(solution)/shard_map/coupled/pallas_call | solution.py:554
  33.9 1.9 %copy.18 = f32[72,16,128]{2,1,0:T(8,128)} copy(f32[72,16,128]{2,1,0:T(8,128)} %bitcast.14) | data formatting | bytes 1179648
  35.9 2.2 %copy.19 = f32[60,16,256]{2,1,0:T(8,128)} copy(f32[60,16,256]{2,1,0:T(8,128)} %bitcast.12) | data formatting | bytes 1966080
  38.1 1.4 %copy.20 = bf16[8,16,128]{2,1,0:T(8,128)(2,1)} copy(bf16[8,16,128]{2,1,0:T(8,128)(2,1)} %bitcast.16) | data formatting | bytes 65536
